TPU v7x, 512 devices: a whole 4x4x16 slice. The times are simulated.
512 devices in a mesh: grp: 16 (over x, y), occ: 32 (over z, core).
Axes of the slice: x: 4, y: 4, z: 16, core: 2. Of those that a mesh axis runs over, the one named last changes fastest.
Arguments:
- b_ints: bfloat16 [4096, 768, 256], P(('grp', 'occ')), may hold values from -6 to 6
- osv_vecs: bfloat16 [4096, 768, 128], P(('grp', 'occ')), may hold values from -0.21875 to 0.21875
- inv_denom: float32 [4096, 128], P(('grp', 'occ')), may hold values from 0.5 to 4
- domains: int32 [4096, 6], P('grp'), may hold values from 0 to 95, all different within a row
- dom_count: int32 [4096], P('grp'), may hold values from 1 to 6
- owner_slot: int32 [96], replicated, may hold values from 0 to 95, each once
Outputs:
- gamma_tiles: bfloat16 [256, 96, 128], P('occ', 'grp')
Inputs may be any that keep to these rules, and one draw needn't show every extreme that they name: `domains`: each row names distinct tiles.
All inputs are finite; a program needn't handle non-finite values.
Results may differ from a plain program's by a relative error of at most 0.0056.
Values may be sent and summed in bfloat16 or wider, within the bound.
No kernel may reach another device: no remote copies, remote signals or barrier semaphores. Data moves between devices by JAX's collectives and lax.ppermute only.
A program may use at most 64 MiB of HBM per device.

v0:
```python
import jax
import jax.numpy as jnp
from jax import lax
from jax.sharding import PartitionSpec as P


def local(b_ints, osv_vecs, inv_denom, domains, dom_count, owner_slot):
    own = b_ints.shape[0]
    kdom = domains.shape[1]
    tile = b_ints.shape[1] // kdom
    ntiles = owner_slot.shape[0]
    tiles_ids = jnp.arange(ntiles, dtype=jnp.int32)
    keep_all = jnp.arange(kdom, dtype=jnp.int32)[None, :] < dom_count[:, None]
    looked = jnp.sum(jnp.where(domains[:, :, None] == tiles_ids, owner_slot, 0), axis=-1)
    slot_all = jnp.where(keep_all, looked, -1)
    start = lax.axis_index("occ") * own
    keep = lax.dynamic_slice_in_dim(keep_all, start, own, 0)
    rowmask = jnp.repeat(keep, tile, axis=1).astype(jnp.bfloat16)
    masked = b_ints * rowmask[:, :, None]
    hidden = jnp.einsum("ikn,ikp->inp", osv_vecs, masked, preferred_element_type=jnp.float32)
    scaled = (hidden * inv_denom[:, :, None]).astype(jnp.bfloat16)
    amp = jnp.einsum("ikn,inp->pik", osv_vecs, scaled, preferred_element_type=jnp.float32)
    amp = (amp * rowmask[None].astype(jnp.float32)).astype(jnp.bfloat16)
    got = lax.all_to_all(amp, "occ", split_axis=0, concat_axis=1, tiled=True)
    inst = got.reshape(got.shape[0], -1, tile)
    onehot = (slot_all.reshape(-1)[None, :] == tiles_ids[:, None]).astype(jnp.bfloat16)
    partial_sum = jnp.einsum("sn,pna->psa", onehot, inst, preferred_element_type=jnp.float32)
    summed = lax.psum_scatter(partial_sum, "grp", scatter_dimension=1, tiled=True)
    return summed.astype(jnp.bfloat16)


def solution(mesh):
    return jax.shard_map(
        local,
        mesh=mesh,
        in_specs=(
            P(("grp", "occ"), None, None),
            P(("grp", "occ"), None, None),
            P(("grp", "occ"), None),
            P("grp", None),
            P("grp"),
            P(),
        ),
        out_specs=P("occ", "grp", None),
        check_vma=False,
    )
```

profile of v0, /device:TPU:6, one launch (start us, length us, event | category | flops | bytes accessed | tf_op | source)
XLA Modules:
  0.0 281.5 jit_solution(14874396371674101723)
XLA Ops:
  6.5 0.0 copy-start
  6.5 0.8 iota_compare_fusion.2
  7.3 0.1 dynamic-slice_convert_fusion
  7.4 0.1 broadcast_bitcast_fusion
  7.5 0.5 copy-done
  8.0 5.6 %fusion = bf16[256,8,768]{2,0,1:T(8,128)(2,1)} fusion(f32[8,768]{1,0:T(8,128)S(1)} %get-tuple-element.6, bf16[8,768,128]{2,1,0:T(8,128)(2,1)S(1)} %copy-done, bf16[8,768,256]{2,1,0:T(8,128)(2,1)} %param.6, bf16[8,768]{1,0:T(8,128)(2,1)S(1)} %get-tuple-element.5, f32[8,128]{1,0:T(8,128)} %param.8), kind=kOutput, calls=%fused_computation.1 | convolution fusion | flops 810549248 | bytes 7905280 | tf_op jit(solution)/shard_map/ikn,inp->pik/dot_general | solution.py:22
  13.6 5.3 %copy.21 = bf16[256,8,768]{2,1,0:T(8,128)(2,1)} copy(bf16[256,8,768]{2,0,1:T(8,128)(2,1)} %fusion) | data formatting | bytes 6291456 | tf_op jit(solution)/shard_map/convert_element_type | solution.py:23
  18.9 0.0 copy-start.1
  18.9 0.0 copy-start.3
  18.9 0.0 copy-start.2
  18.9 15.7 %all-to-all-start = ((bf16[256,8,768]{2,1,0:T(8,128)(2,1)}), bf16[256,8,768]{2,1,0:T(8,128)(2,1)}, u32[]{:S(2)}, u32[]{:S(2)}) async-start(bf16[256,8,768]{2,1,0:T(8,128)(2,1)} %copy.21), calls=%async_computation | async-start | bytes 6291456 | tf_op jit(solution)/shard_map/all_to_all | solution.py:24
  34.6 0.0 reduce-scatter.4.cloned.1.call-start
  34.7 0.0 copy-done.1
  34.7 0.0 copy-done.3
  34.7 0.2 select_reduce_fusion
  34.9 0.0 copy-done.2
  34.9 0.1 copy.23
  35.0 0.1 select_n.21
  35.2 141.0 %all-to-all-done = bf16[256,8,768]{2,1,0:T(8,128)(2,1)} async-done(((bf16[256,8,768]{2,1,0:T(8,128)(2,1)}), bf16[256,8,768]{2,1,0:T(8,128)(2,1)}, u32[]{:S(2)}, u32[]{:S(2)}) %all-to-all-start) | async-done | bytes 3145760 | tf_op jit(solution)/shard_map/all_to_all | solution.py:24
  176.2 3.8 %copy.27 = bf16[32,8,8,768]{3,2,0,1:T(8,128)(2,1)} copy(bf16[32,8,8,768]{3,2,1,0:T(8,128)(2,1)} %bitcast.2) | data formatting | bytes 6291456 | tf_op jit(solution)/shard_map/all_to_all | solution.py:24
  180.0 6.4 %reshape.42 = bf16[8,1536,128]{2,1,0:T(8,128)(2,1)} reshape(bf16[8,32,8,768]{3,2,1,0:T(8,128)(2,1)} %bitcast.20) | data formatting | bytes 6291456 | tf_op jit(solution)/shard_map/reshape | solution.py:25
  186.3 2.5 convolution_bitcast_fusion
  188.8 1.0 copy.24
  189.8 0.0 reduce-scatter.4.cloned.1.call-update
  189.9 83.4 %reduce-scatter.4.cloned.1.call-done = f32[8,6,128]{2,0,1:T(8,128)} async-done(((f32[8,96,128]{2,0,1:T(8,128)}), f32[8,6,128]{2,0,1:T(8,128)}) %reduce-scatter.4.cloned.1.call-update) | async-done | bytes 24592
  273.3 1.3 convert_element_type.43
  (1 shorter events, 0.0 us)
Async XLA Ops:
  6.5 1.4 copy-start
  18.9 15.8 %copy-start.1 = (s32[256,6]{0,1:T(8,128)S(1)}, s32[256,6]{0,1:T(8,128)}, u32[]{:S(2)}) copy-start(s32[256,6]{0,1:T(8,128)} %param.9) | copy-start | bytes 18436
  18.9 15.8 %copy-start.3 = (s32[96]{0:T(128)S(1)}, s32[96]{0:T(128)}, u32[]{:S(2)}) copy-start(s32[96]{0:T(128)} %param.11) | copy-start | bytes 1156
  18.9 16.0 %copy-start.2 = (s32[256]{0:T(256)S(1)}, s32[256]{0:T(256)}, u32[]{:S(2)}) copy-start(s32[256]{0:T(256)} %param.10) | copy-start | bytes 3076
  18.9 157.3 %all-to-all-start = ((bf16[256,8,768]{2,1,0:T(8,128)(2,1)}), bf16[256,8,768]{2,1,0:T(8,128)(2,1)}, u32[]{:S(2)}, u32[]{:S(2)}) async-start(bf16[256,8,768]{2,1,0:T(8,128)(2,1)} %copy.21), calls=%async_computation | async-start | bytes 6291456 | tf_op jit(solution)/shard_map/all_to_all | solution.py:24
  34.6 238.6 %reduce-scatter.4.cloned.1.call-start = ((), (), s32[]{:S(2)}) async-start(), calls=%async_computation.2 | async-start | bytes 417792
Sparse Core Ops, SparseCore 0:
  190.0 83.2 reduce-scatter.3
where the time goes:
time: 282 us; the launch traced here: 281 us
  waiting for transfers between devices  224 us (79%)
  local copies, waits for them, and re-layouts  17.2 us (6%)
  starting transfers between devices  15.8 us (6%)
  between operations  13.5 us (5%)
  matrix products  8.16 us (3%)
    all_to_all x1, waiting for transfers between devices, local(): got = lax.all_to_all(amp, 'occ', split_axis=0, concat_axis=1, tiled=True)  141 us
    unnamed x2, waiting for transfers between devices  83.4 us
    all_to_all x1, starting transfers between devices, local(): got = lax.all_to_all(amp, 'occ', split_axis=0, concat_axis=1, tiled=True)  15.7 us
    reshape x1, local copies, waits for them, and re-layouts, local(): inst = got.reshape(got.shape[0], -1, tile)  6.37 us
    dot_general x1, matrix products, local(): jnp.einsum('ikn,inp->pik', osv_vecs, scaled, preferred_element_type=jnp.f...  5.64 us
  transfers between devices with their start and end apart: 2, of which 2 were waited for; matrix products, arithmetic and copies ran while one was open for 0% of the time, Pallas kernels for 0%

commit v1 on v0

v1 whole, which is shorter than its diff:
```python
import functools

import jax
import jax.numpy as jnp
from jax import lax
from jax.experimental import pallas as pl
from jax.experimental.pallas import tpu as pltpu
from jax.sharding import PartitionSpec as P

LANES = 8


def amplitudes(kdom, tile, cnt_ref, core_ref, b_ref, q_ref, inv_ref, keep_ref, send_ref):
    i = pl.program_id(0)
    used = cnt_ref[i] * tile
    q = q_ref[0]
    rows = lax.broadcasted_iota(jnp.int32, q.shape, 0)
    q = jnp.where(rows < used, q.astype(jnp.float32), 0.0)
    qt = q.T.astype(jnp.bfloat16)
    h = jnp.dot(qt, b_ref[0], preferred_element_type=jnp.float32)
    ht = h.T * inv_ref[pl.ds(i, 1), :]
    nb, nosv = ht.shape
    ht = ht.reshape(nb // (2 * LANES), 2, LANES, nosv)
    even = ht[:, 0].reshape(nb // 2, nosv)
    odd = ht[:, 1].reshape(nb // 2, nosv)
    first = core_ref[0] == 0
    scaled = jnp.concatenate([jnp.where(first, even, odd), jnp.where(first, odd, even)], 0)
    y = jnp.dot(scaled.astype(jnp.bfloat16), qt, preferred_element_type=jnp.float32)
    y = y.astype(jnp.bfloat16)
    for k in range(kdom):
        keep_ref[k] = y[: nb // 2, k * tile : (k + 1) * tile]
        send_ref[k] = y[nb // 2 :, k * tile : (k + 1) * tile]


def combine(own_slots, got_slots, own_ref, got_ref, out_ref, own_head, own_next, got_head, got_next):
    step = pl.program_id(0)
    block = out_ref.shape[0]
    shape = out_ref.shape[1:]

    @pl.when(step == 0)
    def _():
        for slots, head, link in ((own_slots, own_head, own_next), (got_slots, got_head, got_next)):

            @pl.loop(0, head.shape[0])
            def _(s):
                head[s] = -1

            @pl.loop(0, link.shape[0])
            def _(t):
                s = slots[t]

                @pl.when(s >= 0)
                def _():
                    link[t] = head[s]
                    head[s] = t

    def walk(head, link, ref, slot, total):
        def body(state):
            t, total = state
            return link[t], total + ref[t].astype(jnp.float32)

        return lax.while_loop(lambda state: state[0] >= 0, body, (head[slot], total))[1]

    @pl.loop(0, block)
    def _(j):
        slot = step * block + j
        total = walk(own_head, own_next, own_ref, slot, jnp.zeros(shape, jnp.float32))
        out_ref[j] = walk(got_head, got_next, got_ref, slot, total).astype(out_ref.dtype)


def local(ngrp, nocc, b_ints, osv_vecs, inv_denom, domains, dom_count, owner_slot):
    own, rows, nb = b_ints.shape
    kdom = domains.shape[1]
    tile = rows // kdom
    nosv = osv_vecs.shape[2]
    ntiles = owner_slot.shape[0]
    me = lax.axis_index("occ")
    core = me % 2
    half = nb // 2

    pair = lax.dynamic_slice_in_dim(domains, (me - core) * own, 2 * own, 0)
    counts = lax.dynamic_slice_in_dim(dom_count, (me - core) * own, 2 * own, 0)
    keep = jnp.arange(kdom, dtype=jnp.int32)[None, :] < counts[:, None]
    looked = jnp.sum(jnp.where(pair[:, :, None] == jnp.arange(ntiles, dtype=jnp.int32), owner_slot, 0), axis=-1)
    slots = jnp.where(keep, looked, -1).reshape(2, own * kdom)
    own_slots = lax.dynamic_index_in_dim(slots, core, 0, keepdims=False)
    got_slots = lax.dynamic_index_in_dim(slots, 1 - core, 0, keepdims=False)
    own_counts = lax.dynamic_slice_in_dim(dom_count, me * own, own, 0)

    half_tiles = jax.ShapeDtypeStruct((own * kdom, half, tile), jnp.bfloat16)
    kept, sent = pl.pallas_call(
        functools.partial(amplitudes, kdom, tile),
        grid_spec=pltpu.PrefetchScalarGridSpec(
            num_scalar_prefetch=2,
            grid=(own,),
            in_specs=[
                pl.BlockSpec((1, rows, nb), lambda i, *_: (i, 0, 0)),
                pl.BlockSpec((1, rows, nosv), lambda i, *_: (i, 0, 0)),
                pl.BlockSpec((own, nosv), lambda i, *_: (0, 0)),
            ],
            out_specs=[pl.BlockSpec((kdom, half, tile), lambda i, *_: (i, 0, 0))] * 2,
        ),
        out_shape=[half_tiles, half_tiles],
        compiler_params=pltpu.CompilerParams(vmem_limit_bytes=40 << 20),
        cost_estimate=pl.CostEstimate(flops=4 * own * rows * nb * nosv, bytes_accessed=8 << 20, transcendentals=0),
        name="amplitudes",
    )(own_counts, core.reshape(1), b_ints, osv_vecs, inv_denom)

    got = lax.ppermute(sent, "occ", [(i, i ^ 1) for i in range(nocc)])

    block = 12
    whole = pl.BlockSpec((own * kdom, half, tile), lambda g, *_: (0, 0, 0))
    dense = pl.pallas_call(
        combine,
        grid_spec=pltpu.PrefetchScalarGridSpec(
            num_scalar_prefetch=2,
            grid=(ntiles // block,),
            in_specs=[whole, whole],
            out_specs=pl.BlockSpec((block, half, tile), lambda g, *_: (g, 0, 0)),
            scratch_shapes=[
                pltpu.SMEM((ntiles,), jnp.int32),
                pltpu.SMEM((own * kdom,), jnp.int32),
                pltpu.SMEM((ntiles,), jnp.int32),
                pltpu.SMEM((own * kdom,), jnp.int32),
            ],
        ),
        out_shape=jax.ShapeDtypeStruct((ntiles, half, tile), jnp.bfloat16),
        compiler_params=pltpu.CompilerParams(vmem_limit_bytes=40 << 20),
        cost_estimate=pl.CostEstimate(flops=1 << 22, bytes_accessed=7 << 20, transcendentals=0),
        name="combine",
    )(own_slots, got_slots, kept, got)

    parts = lax.all_to_all(dense, "grp", 0, 0, tiled=True)
    mine = parts.reshape(ngrp, ntiles // ngrp, half, tile).astype(jnp.float32).sum(0).astype(jnp.bfloat16)

    nz = nocc // 2
    columns = [[2 * z + c for z in range(nz)] for c in range(2)]
    blocks = mine.reshape(ntiles // ngrp, nz, LANES, tile).transpose(1, 0, 2, 3)
    parts = lax.all_to_all(blocks, "occ", 0, 0, tiled=True, axis_index_groups=columns)
    return parts.astype(jnp.float32).sum(0).astype(jnp.bfloat16).transpose(1, 0, 2)


def solution(mesh):
    return jax.shard_map(
        functools.partial(local, mesh.shape["grp"], mesh.shape["occ"]),
        mesh=mesh,
        in_specs=(
            P(("grp", "occ"), None, None),
            P(("grp", "occ"), None, None),
            P(("grp", "occ"), None),
            P("grp", None),
            P("grp"),
            P(),
        ),
        out_specs=P("occ", "grp", None),
        check_vma=False,
    )
```

time: 282 us -> 101 us (0.36)
  waiting for transfers between devices: 224 us -> 2.63 us
  blocking collectives: 0 us -> 75.6 us
  starting transfers between devices: 15.8 us -> 1.91 us
  between operations: 13.5 us -> 0.09 us
  Pallas kernels: 0 us -> 11.9 us
  local copies, waits for them, and re-layouts: 17.2 us -> 5.44 us
  matrix products: 8.16 us -> 0 us
    all_to_all x1 -> x0, waiting for transfers between devices: 141 us -> none  [local(): got = lax.all_to_all(amp, 'occ', split_axis=0, concat_axis=1, tiled=True)]
    unnamed x2 -> x0, waiting for transfers between devices: 83.4 us -> none
    all_to_all x0 -> x2, blocking collectives: none -> 75.6 us  [the longest x1 46.4 us: local(): parts = lax.all_to_all(dense, 'grp', 0, 0, tiled=True)]
    all_to_all x1 -> x0, starting transfers between devices: 15.7 us -> none  [local(): got = lax.all_to_all(amp, 'occ', split_axis=0, concat_axis=1, tiled=True)]
    pallas_call x0 -> x2, Pallas kernels: none -> 11.9 us  [the longest x1 6.51 us: local(): pl.pallas_call(functools.partial(amplitudes, kdom, tile), grid_spec=pltpu...]
    dot_general x2 -> x0, matrix products: 8.16 us -> none  [the longest x1 5.64 us: local(): jnp.einsum('ikn,inp->pik', osv_vecs, scaled, preferred_element_type=jnp.f...]
    reshape x1 -> x0, local copies, waits for them, and re-layouts: 6.37 us -> none  [local(): inst = got.reshape(got.shape[0], -1, tile)]
    convert_element_type x1 -> x0, local copies, waits for them, and re-layouts: 5.3 us -> none  [local(): amp = (amp * rowmask[None].astype(jnp.float32)).astype(jnp.bfloat16)]
  transfers between devices with their start and end apart: 2 -> 1, of which waited for: 2 -> 1; matrix products, arithmetic and copies ran while one was open for 0% -> 1% of each run, Pallas kernels for 0% -> 0%
where the time goes in v1:
time: 101 us; the launch traced here: 99.1 us
  blocking collectives  75.6 us (75%)
  Pallas kernels  11.9 us (12%)
  local copies, waits for them, and re-layouts  5.44 us (5%)
  waiting for transfers between devices  2.63 us (3%)
  starting transfers between devices  1.91 us (2%)
  other arithmetic  1.51 us (1%)
    all_to_all x1, blocking collectives, local(): parts = lax.all_to_all(dense, 'grp', 0, 0, tiled=True)  46.4 us
    all_to_all x1, blocking collectives, local(): lax.all_to_all(blocks, 'occ', 0, 0, tiled=True, axis_index_groups=columns)  29.2 us
    pallas_call x1, Pallas kernels, local(): pl.pallas_call(functools.partial(amplitudes, kdom, tile), grid_spec=pltpu...  6.51 us
    pallas_call x1, Pallas kernels, local(): pl.pallas_call(combine, grid_spec=pltpu.PrefetchScalarGridSpec(num_scalar...  5.43 us
    unnamed x12, local copies, waits for them, and re-layouts  3.99 us
    ppermute x1, waiting for transfers between devices, local(): got = lax.ppermute(sent, 'occ', [(i, i ^ 1) for i in range(nocc)])  2.63 us
  transfers between devices with their start and end apart: 1, of which 1 were waited for; matrix products, arithmetic and copies ran while one was open for 1% of the time, Pallas kernels for 0%

profile of v1, /device:TPU:6, one launch (start us, length us, event | category | flops | bytes accessed | tf_op | source)
XLA Modules:
  0.0 99.1 jit_solution(11772792003688255933)
XLA Ops:
  0.0 0.0 copy-start
  0.0 0.8 dynamic_slice.20.cnt_ref
  0.8 0.0 copy-start.1
  0.8 1.9 %copy-done.1 = bf16[8,768,256]{2,1,0:T(8,128)(2,1)S(1)} copy-done((bf16[8,768,256]{2,1,0:T(8,128)(2,1)S(1)}, bf16[8,768,256]{2,1,0:T(8,128)(2,1)}, u32[]{:S(2)}) %copy-start.1) | copy-done | bytes 3145752
  2.7 0.0 copy-start.2
  2.7 1.4 %copy-done.2 = bf16[8,768,128]{2,1,0:T(8,128)(2,1)S(1)} copy-done((bf16[8,768,128]{2,1,0:T(8,128)(2,1)S(1)}, bf16[8,768,128]{2,1,0:T(8,128)(2,1)}, u32[]{:S(2)}) %copy-start.2) | copy-done | bytes 1572888
  4.1 0.0 copy-start.3
  4.1 0.7 copy-done.3
  4.8 0.0 copy-start.5
  4.8 0.0 copy-start.4
  4.8 6.5 %amplitudes.1 = (bf16[48,128,128]{2,1,0:T(8,128)(2,1)S(1)}, bf16[48,128,128]{2,1,0:T(8,128)(2,1)}) custom-call(s32[8]{0:T(128)S(1)} %dynamic_slice.20.cnt_ref, s32[1]{0:T(128)} %bitcast.2.core_ref, bf16[8,768,256]{2,1,0:T(8,128)(2,1)S(1)} %copy-done.1, bf16[8,768,128]{2,1,0:T(8,128)(2,1)S(1)} %copy-done.2, f32[8,128]{1,0:T(8,128)S(1)} %copy-done.3), custom_call_target="tpu_custom_call" | custom-call | flops 805306368 | bytes 8388608 | tf_op jit(solution)/shard_map/amplitudes/pallas_call | solution.py:91
  11.3 1.9 %collective-permute-start = (bf16[48,128,128]{2,1,0:T(8,128)(2,1)}, bf16[48,128,128]{2,1,0:T(8,128)(2,1)S(1)}, u32[]{:S(2)}, u32[]{:S(2)}) collective-permute-start(bf16[48,128,128]{2,1,0:T(8,128)(2,1)} %get-tuple-element.8), channel_id=1, source_target_pairs={{0,1},{1,0},{2,3},{3,2},{4,5},{5,4},{6,7},{7,6},{8,9},{9,8},{10,11... | collective-permute-start | bytes 4718600 | tf_op jit(solution)/shard_map/ppermute | solution.py:109
  13.2 0.0 copy-done.5
  13.2 0.1 dynamic_slice.16
  13.3 0.1 lt.47
  13.4 0.0 copy-done
  13.4 0.1 constant_dynamic-slice_fusion.2
  13.5 0.0 copy-done.4
  13.5 0.2 select_reduce_fusion
  13.7 0.1 copy.12
  13.8 0.1 reduce_sum.36
  13.9 0.1 lt.43
  14.0 0.1 lt.48
  14.0 0.1 lt.49
  14.1 2.6 %collective-permute-done.got_ref = bf16[48,128,128]{2,1,0:T(8,128)(2,1)S(1)} collective-permute-done((bf16[48,128,128]{2,1,0:T(8,128)(2,1)}, bf16[48,128,128]{2,1,0:T(8,128)(2,1)S(1)}, u32[]{:S(2)}, u32[]{:S(2)}) %collective-permute-start) | collective-permute-done | bytes 1572896 | tf_op jit(solution)/shard_map/ppermute | solution.py:109
  16.8 5.4 %combine.1 = bf16[96,128,128]{2,1,0:T(8,128)(2,1)S(1)} custom-call(s32[48]{0:T(128)S(1)} %get-tuple-element.10.own_slots, s32[48]{0:T(128)S(1)} %get-tuple-element.9.got_slots, bf16[48,128,128]{2,1,0:T(8,128)(2,1)S(1)} %get-tuple-element.7.own_ref, bf16[48,128,128]{2,1,0:T(8,128)(2,1)S(1)} %collective-permute-done.got_ref), custom_call_target="tpu_custom_call" | custom-call | flops 4194304 | bytes 7340032 | tf_op jit(solution)/shard_map/combine/pallas_call | solution.py:113
  22.2 46.4 %all_to_all.10 = bf16[96,128,128]{2,1,0:T(8,128)(2,1)S(1)} all-to-all(bf16[96,128,128]{2,1,0:T(8,128)(2,1)S(1)} %combine.1), channel_id=1, replica_groups=mesh['grp'=16,'occ'=32] {'grp'}, dimensions={0} | all-to-all | bytes 6291456 | tf_op jit(solution)/shard_map/all_to_all | solution.py:133
  68.6 0.6 reduce_sum.37
  69.3 29.2 %all_to_all.11 = bf16[16,6,8,128]{3,2,1,0:T(8,128)(2,1)S(1)} all-to-all(bf16[16,6,8,128]{3,2,1,0:T(8,128)(2,1)S(1)} %copy.13), channel_id=1, replica_groups={{0,2,4,6,8,10,12,14,16,18,20,22,24,26,28,30},{1,3,5,7,9,11,13,15,17,19,..., dimensions={0} | all-to-all | bytes 393216 | tf_op jit(solution)/shard_map/all_to_all | solution.py:139
  98.5 0.6 reduce_sum.38
  (4 shorter events, 0.1 us)
Async XLA Ops:
  0.0 13.4 %copy-start = (s32[256,6]{0,1:T(8,128)S(1)}, s32[256,6]{0,1:T(8,128)}, u32[]{:S(2)}) copy-start(s32[256,6]{0,1:T(8,128)} %param.9) | copy-start | bytes 18436
  0.8 1.9 %copy-start.1 = (bf16[8,768,256]{2,1,0:T(8,128)(2,1)S(1)}, bf16[8,768,256]{2,1,0:T(8,128)(2,1)}, u32[]{:S(2)}) copy-start(bf16[8,768,256]{2,1,0:T(8,128)(2,1)} %b_ref.1) | copy-start | bytes 9437188
  2.7 1.4 %copy-start.2 = (bf16[8,768,128]{2,1,0:T(8,128)(2,1)S(1)}, bf16[8,768,128]{2,1,0:T(8,128)(2,1)}, u32[]{:S(2)}) copy-start(bf16[8,768,128]{2,1,0:T(8,128)(2,1)} %q_ref.1) | copy-start | bytes 4718596
  4.1 0.7 copy-start.3
  4.8 8.5 %copy-start.5 = (s32[256]{0:T(256)S(1)}, s32[256]{0:T(256)}, u32[]{:S(2)}) copy-start(s32[256]{0:T(256)} %param.10) | copy-start | bytes 3076
  4.8 8.7 %copy-start.4 = (s32[96]{0:T(128)S(1)}, s32[96]{0:T(128)}, u32[]{:S(2)}) copy-start(s32[96]{0:T(128)} %param.11) | copy-start | bytes 1156
  11.3 5.5 %collective-permute-start = (bf16[48,128,128]{2,1,0:T(8,128)(2,1)}, bf16[48,128,128]{2,1,0:T(8,128)(2,1)S(1)}, u32[]{:S(2)}, u32[]{:S(2)}) collective-permute-start(bf16[48,128,128]{2,1,0:T(8,128)(2,1)} %get-tuple-element.8), channel_id=1, source_target_pairs={{0,1},{1,0},{2,3},{3,2},{4,5},{5,4},{6,7},{7,6},{8,9},{9,8},{10,11... | collective-permute-start | bytes 4718600 | tf_op jit(solution)/shard_map/ppermute | solution.py:109

commit v2 on v0

v2 whole, which is shorter than its diff:
```python
import functools

import jax
import jax.numpy as jnp
from jax import lax
from jax.experimental import pallas as pl
from jax.experimental.pallas import tpu as pltpu
from jax.sharding import PartitionSpec as P

LANES = 8


def amplitudes(kdom, tile, me_ref, cnt_hbm, b_hbm, q_hbm, inv_hbm, keep_hbm, send_hbm, cnt, b_buf, q_buf, inv, keep_ref, send_ref, small, sems):
    own = b_buf.shape[0]
    me = me_ref[0]
    counts = pltpu.make_async_copy(cnt_hbm, cnt, small.at[0])
    counts.start()
    gaps = pltpu.make_async_copy(inv_hbm, inv, small.at[1])
    gaps.start()

    def fetch(i):
        return (
            pltpu.make_async_copy(q_hbm.at[i], q_buf.at[i], sems.at[0, i]),
            pltpu.make_async_copy(b_hbm.at[i], b_buf.at[i], sems.at[1, i]),
        )

    def store(i):
        tiles = pl.ds(i * kdom, kdom)
        return (
            pltpu.make_async_copy(keep_ref.at[tiles], keep_hbm.at[tiles], sems.at[2, i]),
            pltpu.make_async_copy(send_ref.at[tiles], send_hbm.at[tiles], sems.at[3, i]),
        )

    for i in range(own):
        for copy in fetch(i):
            copy.start()
    counts.wait()
    gaps.wait()
    first = me % 2 == 0

    @pl.loop(0, own)
    def _(i):
        for copy in fetch(i):
            copy.wait()
        used = cnt[me * own + i]
        row = inv[pl.ds(i, 1), :]

        def part(tiles):
            rows = tiles * tile
            q = q_buf[i, :rows]
            at = lax.broadcasted_iota(jnp.int32, q.shape, 0)
            masked = jnp.where(at < used * tile, q.astype(jnp.float32), 0.0).astype(jnp.bfloat16)
            h = lax.dot_general(b_buf[i, :rows], masked, (((0,), (0,)), ((), ())), preferred_element_type=jnp.float32)
            h = h * row
            nb, nosv = h.shape
            h = h.reshape(nb // (2 * LANES), 2, LANES, nosv)
            even = h[:, 0].reshape(nb // 2, nosv)
            odd = h[:, 1].reshape(nb // 2, nosv)
            scaled = jnp.concatenate([jnp.where(first, even, odd), jnp.where(first, odd, even)], 0)
            y = lax.dot_general(
                scaled.astype(jnp.bfloat16), q, (((1,), (1,)), ((), ())), preferred_element_type=jnp.float32
            ).astype(jnp.bfloat16)
            for k in range(tiles):
                keep_ref[i * kdom + k] = y[: nb // 2, k * tile : (k + 1) * tile]
                send_ref[i * kdom + k] = y[nb // 2 :, k * tile : (k + 1) * tile]

        for low in range(0, kdom, 2):
            high = min(low + 2, kdom)
            inside = used > low if high == kdom else jnp.logical_and(used > low, used <= high)
            pl.when(inside)(functools.partial(part, high))
        for copy in store(i):
            copy.start()

    @pl.loop(0, own)
    def _(i):
        for copy in store(i):
            copy.wait()


def combine(slot_ref, next_ref, own_ref, got_ref, out_ref):
    half = own_ref.shape[0]
    tiles = 2 * half
    out_ref[...] = jnp.zeros_like(out_ref)

    def tile(t):
        a = own_ref[jnp.minimum(t, half - 1)].astype(jnp.float32)
        b = got_ref[jnp.maximum(t - half, 0)].astype(jnp.float32)
        return jnp.where(t < half, a, b)

    def enter(ref, offset):
        @pl.loop(0, half)
        def _(t):
            slot = slot_ref[t + offset]

            @pl.when(slot >= 0)
            def _():
                after = next_ref[t + offset]

                @pl.when(after >= tiles)
                def _():
                    out_ref[slot] = ref[t]

                @pl.when(after < tiles)
                def _():
                    def body(state):
                        n, total = state
                        return next_ref[n], total + tile(n)

                    total = lax.while_loop(lambda state: state[0] < tiles, body, (after, ref[t].astype(jnp.float32)))[1]
                    out_ref[slot] = total.astype(out_ref.dtype)

    enter(own_ref, 0)
    enter(got_ref, half)


def local(ngrp, nocc, b_ints, osv_vecs, inv_denom, domains, dom_count, owner_slot):
    own, rows, nb = b_ints.shape
    kdom = domains.shape[1]
    tile = rows // kdom
    nosv = osv_vecs.shape[2]
    ntiles = owner_slot.shape[0]
    me = lax.axis_index("occ")
    core = me % 2
    half = nb // 2
    vmem = pl.BlockSpec(memory_space=pltpu.VMEM)
    smem = pl.BlockSpec(memory_space=pltpu.SMEM)
    hbm = pl.BlockSpec(memory_space=pl.ANY)

    half_tiles = jax.ShapeDtypeStruct((own * kdom, half, tile), jnp.bfloat16)
    kept, sent = pl.pallas_call(
        functools.partial(amplitudes, kdom, tile),
        in_specs=[smem, hbm, hbm, hbm, hbm],
        out_specs=[hbm, hbm],
        out_shape=[half_tiles, half_tiles],
        scratch_shapes=[
            pltpu.SMEM(dom_count.shape, jnp.int32),
            pltpu.VMEM(b_ints.shape, b_ints.dtype),
            pltpu.VMEM(osv_vecs.shape, osv_vecs.dtype),
            pltpu.VMEM(inv_denom.shape, inv_denom.dtype),
            pltpu.VMEM(half_tiles.shape, half_tiles.dtype),
            pltpu.VMEM(half_tiles.shape, half_tiles.dtype),
            pltpu.SemaphoreType.DMA((2,)),
            pltpu.SemaphoreType.DMA((4, own)),
        ],
        compiler_params=pltpu.CompilerParams(vmem_limit_bytes=60 << 20),
        cost_estimate=pl.CostEstimate(flops=4 * own * rows * nb * nosv, bytes_accessed=8 << 20, transcendentals=0),
        name="amplitudes",
    )(me.reshape(1), dom_count, b_ints, osv_vecs, inv_denom)

    got = lax.ppermute(sent, "occ", [(i, i ^ 1) for i in range(nocc)])

    base = (me - core) * own
    pair = lax.dynamic_slice_in_dim(domains, base, 2 * own, 0)
    counts = lax.dynamic_slice_in_dim(dom_count, base, 2 * own, 0)
    keep = jnp.arange(kdom, dtype=jnp.int32)[None, :] < counts[:, None]
    looked = jnp.sum(jnp.where(pair[:, :, None] == jnp.arange(ntiles, dtype=jnp.int32), owner_slot, 0), axis=-1)
    slots = jnp.where(keep, looked, -1)
    slots = jnp.where(core == 0, slots, jnp.roll(slots, own, axis=0)).reshape(-1)
    count = slots.shape[0]
    order = jnp.arange(count, dtype=jnp.int32)
    same = slots[:, None] == slots[None, :]
    earlier = jnp.any(same & (order[None, :] < order[:, None]), axis=1)
    heads = jnp.where(earlier, -1, slots)
    after = jnp.min(jnp.where(same & (order[None, :] > order[:, None]), order[None, :], count), axis=1)

    dense = pl.pallas_call(
        combine,
        in_specs=[smem, smem, vmem, vmem],
        out_specs=vmem,
        out_shape=jax.ShapeDtypeStruct((ntiles, half, tile), jnp.bfloat16),
        compiler_params=pltpu.CompilerParams(vmem_limit_bytes=24 << 20),
        cost_estimate=pl.CostEstimate(flops=1 << 22, bytes_accessed=7 << 20, transcendentals=0),
        name="combine",
    )(heads, after, kept, got)

    parts = lax.all_to_all(dense, "grp", 0, 0, tiled=True)
    mine = parts.reshape(ngrp, ntiles // ngrp, half, tile).astype(jnp.float32).sum(0).astype(jnp.bfloat16)

    nz = nocc // 2
    columns = [[2 * z + c for z in range(nz)] for c in range(2)]
    blocks = mine.reshape(ntiles // ngrp, nz, LANES, tile).transpose(1, 0, 2, 3)
    parts = lax.all_to_all(blocks, "occ", 0, 0, tiled=True, axis_index_groups=columns)
    return parts.astype(jnp.float32).sum(0).astype(jnp.bfloat16).transpose(1, 0, 2)


def solution(mesh):
    return jax.shard_map(
        functools.partial(local, mesh.shape["grp"], mesh.shape["occ"]),
        mesh=mesh,
        in_specs=(
            P(("grp", "occ"), None, None),
            P(("grp", "occ"), None, None),
            P(("grp", "occ"), None),
            P("grp", None),
            P("grp"),
            P(),
        ),
        out_specs=P("occ", "grp", None),
        check_vma=False,
    )
```

time: 282 us -> 95.5 us (0.34)
  waiting for transfers between devices: 224 us -> 2.36 us
  blocking collectives: 0 us -> 76.1 us
  local copies, waits for them, and re-layouts: 17.2 us -> 1.85 us
  starting transfers between devices: 15.8 us -> 1.98 us
  between operations: 13.5 us -> 0.1 us
  Pallas kernels: 0 us -> 9.7 us
  matrix products: 8.16 us -> 0 us
    all_to_all x1 -> x0, waiting for transfers between devices: 141 us -> none  [local(): got = lax.all_to_all(amp, 'occ', split_axis=0, concat_axis=1, tiled=True)]
    unnamed x2 -> x0, waiting for transfers between devices: 83.4 us -> none
    all_to_all x0 -> x2, blocking collectives: none -> 76.1 us  [the longest x1 46.8 us: local(): parts = lax.all_to_all(dense, 'grp', 0, 0, tiled=True)]
    all_to_all x1 -> x0, starting transfers between devices: 15.7 us -> none  [local(): got = lax.all_to_all(amp, 'occ', split_axis=0, concat_axis=1, tiled=True)]
    pallas_call x0 -> x2, Pallas kernels: none -> 9.7 us  [the longest x1 6.78 us: local(): pl.pallas_call(functools.partial(amplitudes, kdom, tile), in_specs=[smem,...]
    dot_general x2 -> x0, matrix products: 8.16 us -> none  [the longest x1 5.64 us: local(): jnp.einsum('ikn,inp->pik', osv_vecs, scaled, preferred_element_type=jnp.f...]
    reshape x1 -> x0, local copies, waits for them, and re-layouts: 6.37 us -> none  [local(): inst = got.reshape(got.shape[0], -1, tile)]
    convert_element_type x1 -> x0, local copies, waits for them, and re-layouts: 5.3 us -> none  [local(): amp = (amp * rowmask[None].astype(jnp.float32)).astype(jnp.bfloat16)]
  transfers between devices with their start and end apart: 2 -> 1, of which waited for: 2 -> 1; matrix products, arithmetic and copies ran while one was open for 0% -> 1% of each run, Pallas kernels for 0% -> 0%
where the time goes in v2:
time: 95.5 us; the launch traced here: 94.1 us
  blocking collectives  76.1 us (80%)
  Pallas kernels  9.7 us (10%)
  waiting for transfers between devices  2.36 us (2%)
  starting transfers between devices  1.98 us (2%)
  other arithmetic  1.95 us (2%)
  local copies, waits for them, and re-layouts  1.85 us (2%)
    all_to_all x1, blocking collectives, local(): parts = lax.all_to_all(dense, 'grp', 0, 0, tiled=True)  46.8 us
    all_to_all x1, blocking collectives, local(): lax.all_to_all(blocks, 'occ', 0, 0, tiled=True, axis_index_groups=columns)  29.4 us
    pallas_call x1, Pallas kernels, local(): pl.pallas_call(functools.partial(amplitudes, kdom, tile), in_specs=[smem,...  6.78 us
    pallas_call x1, Pallas kernels, local(): pl.pallas_call(combine, in_specs=[smem, smem, vmem, vmem], out_specs=vmem...  2.92 us
    ppermute x1, waiting for transfers between devices, local(): got = lax.ppermute(sent, 'occ', [(i, i ^ 1) for i in range(nocc)])  2.36 us
    ppermute x1, starting transfers between devices, local(): got = lax.ppermute(sent, 'occ', [(i, i ^ 1) for i in range(nocc)])  1.98 us
  transfers between devices with their start and end apart: 1, of which 1 were waited for; matrix products, arithmetic and copies ran while one was open for 1% of the time, Pallas kernels for 0%

profile of v2, /device:TPU:6, one launch (start us, length us, event | category | flops | bytes accessed | tf_op | source)
XLA Modules:
  0.0 94.1 jit_solution(17016758570108607948)
XLA Ops:
  0.0 0.0 copy-start
  0.0 0.0 copy-start.2
  0.0 0.0 copy-start.3
  0.0 6.8 %amplitudes.1 = (bf16[48,128,128]{2,1,0:T(8,128)(2,1)}, bf16[48,128,128]{2,1,0:T(8,128)(2,1)}) custom-call(s32[1]{0:T(128)} %bitcast.me_ref, s32[256]{0:T(256)} %cnt_hbm.1, bf16[8,768,256]{2,1,0:T(8,128)(2,1)} %b_hbm.1, bf16[8,768,128]{2,1,0:T(8,128)(2,1)} %q_hbm.1, f32[8,128]{1,0:T(8,128)} %inv_hbm.1), custom_call_target="tpu_custom_call" | custom-call | flops 805306368 | bytes 8388608 | tf_op jit(solution)/shard_map/amplitudes/pallas_call | solution.py:130
  6.8 2.0 %collective-permute-start = (bf16[48,128,128]{2,1,0:T(8,128)(2,1)}, bf16[48,128,128]{2,1,0:T(8,128)(2,1)S(1)}, u32[]{:S(2)}, u32[]{:S(2)}) collective-permute-start(bf16[48,128,128]{2,1,0:T(8,128)(2,1)} %get-tuple-element.8), channel_id=1, source_target_pairs={{0,1},{1,0},{2,3},{3,2},{4,5},{5,4},{6,7},{7,6},{8,9},{9,8},{10,11... | collective-permute-start | bytes 4718600 | tf_op jit(solution)/shard_map/ppermute | solution.py:150
  8.8 0.0 copy-done.2
  8.8 0.1 dynamic_slice.6
  8.9 0.0 copy-done
  8.9 0.1 constant_dynamic-slice_fusion
  9.0 0.0 copy-done.3
  9.0 0.2 select_reduce_fusion.1
  9.2 0.1 fusion.2
  9.3 0.1 add_select_fusion
  9.4 0.1 copy.12
  9.5 0.1 select_n.63
  9.6 0.2 fusion
  9.7 0.2 select_reduce_fusion.next_ref
  10.0 2.4 %collective-permute-done.got_ref = bf16[48,128,128]{2,1,0:T(8,128)(2,1)S(1)} collective-permute-done((bf16[48,128,128]{2,1,0:T(8,128)(2,1)}, bf16[48,128,128]{2,1,0:T(8,128)(2,1)S(1)}, u32[]{:S(2)}, u32[]{:S(2)}) %collective-permute-start) | collective-permute-done | bytes 1572896 | tf_op jit(solution)/shard_map/ppermute | solution.py:150
  12.3 0.0 copy-start.1
  12.3 1.4 %copy-done.1 = bf16[48,128,128]{2,1,0:T(8,128)(2,1)S(1)} copy-done((bf16[48,128,128]{2,1,0:T(8,128)(2,1)S(1)}, bf16[48,128,128]{2,1,0:T(8,128)(2,1)}, u32[]{:S(2)}) %copy-start.1) | copy-done | bytes 1572888
  13.7 2.9 %combine.1 = bf16[96,128,128]{2,1,0:T(8,128)(2,1)S(1)} custom-call(s32[96]{0:T(128)S(1)} %broadcast_select_fusion.slot_ref, s32[96]{0:T(128)S(1)} %select_reduce_fusion.next_ref, bf16[48,128,128]{2,1,0:T(8,128)(2,1)S(1)} %copy-done.1, bf16[48,128,128]{2,1,0:T(8,128)(2,1)S(1)} %collective-permute-done.got_ref), custom_call_target="tpu_custom_call" | custom-call | flops 4194304 | bytes 7340032 | tf_op jit(solution)/shard_map/combine/pallas_call | solution.py:166
  16.6 46.8 %all_to_all.10 = bf16[96,128,128]{2,1,0:T(8,128)(2,1)S(1)} all-to-all(bf16[96,128,128]{2,1,0:T(8,128)(2,1)S(1)} %combine.1), channel_id=1, replica_groups=mesh['grp'=16,'occ'=32] {'grp'}, dimensions={0} | all-to-all | bytes 6291456 | tf_op jit(solution)/shard_map/all_to_all | solution.py:176
  63.4 0.6 reduce_sum.34
  64.1 29.4 %all_to_all.11 = bf16[16,6,8,128]{3,2,1,0:T(8,128)(2,1)S(1)} all-to-all(bf16[16,6,8,128]{3,2,1,0:T(8,128)(2,1)S(1)} %copy.13), channel_id=1, replica_groups={{0,2,4,6,8,10,12,14,16,18,20,22,24,26,28,30},{1,3,5,7,9,11,13,15,17,19,..., dimensions={0} | all-to-all | bytes 393216 | tf_op jit(solution)/shard_map/all_to_all | solution.py:182
  93.5 0.6 reduce_sum.35
  (3 shorter events, 0.0 us)
Async XLA Ops:
  0.0 8.9 %copy-start = (s32[256,6]{0,1:T(8,128)S(1)}, s32[256,6]{0,1:T(8,128)}, u32[]{:S(2)}) copy-start(s32[256,6]{0,1:T(8,128)} %param.9) | copy-start | bytes 18436
  0.0 8.8 %copy-start.2 = (s32[256]{0:T(256)S(1)}, s32[256]{0:T(256)}, u32[]{:S(2)}) copy-start(s32[256]{0:T(256)} %cnt_hbm.1) | copy-start | bytes 3076
  0.0 9.0 %copy-start.3 = (s32[96]{0:T(128)S(1)}, s32[96]{0:T(128)}, u32[]{:S(2)}) copy-start(s32[96]{0:T(128)} %param.11) | copy-start | bytes 1156
  6.8 5.5 %collective-permute-start = (bf16[48,128,128]{2,1,0:T(8,128)(2,1)}, bf16[48,128,128]{2,1,0:T(8,128)(2,1)S(1)}, u32[]{:S(2)}, u32[]{:S(2)}) collective-permute-start(bf16[48,128,128]{2,1,0:T(8,128)(2,1)} %get-tuple-element.8), channel_id=1, source_target_pairs={{0,1},{1,0},{2,3},{3,2},{4,5},{5,4},{6,7},{7,6},{8,9},{9,8},{10,11... | collective-permute-start | bytes 4718600 | tf_op jit(solution)/shard_map/ppermute | solution.py:150
  12.3 1.4 %copy-start.1 = (bf16[48,128,128]{2,1,0:T(8,128)(2,1)S(1)}, bf16[48,128,128]{2,1,0:T(8,128)(2,1)}, u32[]{:S(2)}) copy-start(bf16[48,128,128]{2,1,0:T(8,128)(2,1)} %get-tuple-element.7.own_ref) | copy-start | bytes 4718596

commit v3 on v2

--- a/solution.py
+++ b/solution.py
@@ -1,4 +1,5 @@
 import functools
+import math
 
 import jax
 import jax.numpy as jnp
@@ -10,7 +11,7 @@
 LANES = 8
 
 
-def amplitudes(kdom, tile, me_ref, cnt_hbm, b_hbm, q_hbm, inv_hbm, keep_hbm, send_hbm, cnt, b_buf, q_buf, inv, keep_ref, send_ref, small, sems):
+def amplitudes(kdom, tile, me_ref, cnt_hbm, b_hbm, q_hbm, inv_hbm, keep_ref, send_hbm, cnt, b_buf, q_buf, inv, send_ref, small, sems):
     own = b_buf.shape[0]
     me = me_ref[0]
     counts = pltpu.make_async_copy(cnt_hbm, cnt, small.at[0])
@@ -26,10 +27,7 @@
 
     def store(i):
         tiles = pl.ds(i * kdom, kdom)
-        return (
-            pltpu.make_async_copy(keep_ref.at[tiles], keep_hbm.at[tiles], sems.at[2, i]),
-            pltpu.make_async_copy(send_ref.at[tiles], send_hbm.at[tiles], sems.at[3, i]),
-        )
+        return pltpu.make_async_copy(send_ref.at[tiles], send_hbm.at[tiles], sems.at[2, i])
 
     for i in range(own):
         for copy in fetch(i):
@@ -68,13 +66,11 @@
             high = min(low + 2, kdom)
             inside = used > low if high == kdom else jnp.logical_and(used > low, used <= high)
             pl.when(inside)(functools.partial(part, high))
-        for copy in store(i):
-            copy.start()
+        store(i).start()
 
     @pl.loop(0, own)
     def _(i):
-        for copy in store(i):
-            copy.wait()
+        store(i).wait()
 
 
 def combine(slot_ref, next_ref, own_ref, got_ref, out_ref):
@@ -130,7 +126,7 @@
     kept, sent = pl.pallas_call(
         functools.partial(amplitudes, kdom, tile),
         in_specs=[smem, hbm, hbm, hbm, hbm],
-        out_specs=[hbm, hbm],
+        out_specs=[vmem, hbm],
         out_shape=[half_tiles, half_tiles],
         scratch_shapes=[
             pltpu.SMEM(dom_count.shape, jnp.int32),
@@ -138,11 +134,10 @@
             pltpu.VMEM(osv_vecs.shape, osv_vecs.dtype),
             pltpu.VMEM(inv_denom.shape, inv_denom.dtype),
             pltpu.VMEM(half_tiles.shape, half_tiles.dtype),
-            pltpu.VMEM(half_tiles.shape, half_tiles.dtype),
             pltpu.SemaphoreType.DMA((2,)),
-            pltpu.SemaphoreType.DMA((4, own)),
+            pltpu.SemaphoreType.DMA((3, own)),
         ],
-        compiler_params=pltpu.CompilerParams(vmem_limit_bytes=60 << 20),
+        compiler_params=pltpu.CompilerParams(vmem_limit_bytes=52 << 20),
         cost_estimate=pl.CostEstimate(flops=4 * own * rows * nb * nosv, bytes_accessed=8 << 20, transcendentals=0),
         name="amplitudes",
     )(me.reshape(1), dom_count, b_ints, osv_vecs, inv_denom)
@@ -153,7 +148,12 @@
     pair = lax.dynamic_slice_in_dim(domains, base, 2 * own, 0)
     counts = lax.dynamic_slice_in_dim(dom_count, base, 2 * own, 0)
     keep = jnp.arange(kdom, dtype=jnp.int32)[None, :] < counts[:, None]
-    looked = jnp.sum(jnp.where(pair[:, :, None] == jnp.arange(ntiles, dtype=jnp.int32), owner_slot, 0), axis=-1)
+    side = math.isqrt(ngrp)
+    each = ntiles // ngrp
+    owner, within = owner_slot // each, owner_slot % each
+    turned = ((owner % side) * side + owner // side) * each + within
+    places = jnp.where(core == 0, owner_slot, turned)
+    looked = jnp.sum(jnp.where(pair[:, :, None] == jnp.arange(ntiles, dtype=jnp.int32), places, 0), axis=-1)
     slots = jnp.where(keep, looked, -1)
     slots = jnp.where(core == 0, slots, jnp.roll(slots, own, axis=0)).reshape(-1)
     count = slots.shape[0]
@@ -173,8 +173,17 @@
         name="combine",
     )(heads, after, kept, got)
 
-    parts = lax.all_to_all(dense, "grp", 0, 0, tiled=True)
-    mine = parts.reshape(ngrp, ntiles // ngrp, half, tile).astype(jnp.float32).sum(0).astype(jnp.bfloat16)
+    def line(along, fixed, z, c):
+        chips = [(t, fixed) if along == 0 else (fixed, t) for t in range(side)]
+        return [(x * side + y) * nocc + 2 * z + c for x, y in chips]
+
+    def stage(tiles, number):
+        groups = [line(number ^ c, fixed, z, c) for c in range(2) for z in range(nocc // 2) for fixed in range(side)]
+        parts = lax.all_to_all(tiles, ("grp", "occ"), 0, 0, tiled=True, axis_index_groups=groups)
+        parts = parts.reshape(side, tiles.shape[0] // side, half, tile)
+        return parts.astype(jnp.float32).sum(0).astype(jnp.bfloat16)
+
+    mine = stage(stage(dense, 0), 1)
 
     nz = nocc // 2
     columns = [[2 * z + c for z in range(nz)] for c in range(2)]

time: 95.5 us -> 88.5 us (0.927)
  blocking collectives: 76.1 us -> 69.4 us
  other arithmetic: 1.95 us -> 3.17 us
  Pallas kernels: 9.7 us -> 8.73 us
    all_to_all x1 -> x2, blocking collectives: 46.8 us -> 41.3 us  [stage(): lax.all_to_all(tiles, ('grp', 'occ'), 0, 0, tiled=True, axis_index_groups...]
    all_to_all x1, blocking collectives: 29.4 us -> 28.2 us  [local(): lax.all_to_all(blocks, 'occ', 0, 0, tiled=True, axis_index_groups=columns)]
    reduce_sum x1 -> x2, other arithmetic: 0.62 us -> 1.82 us  [stage(): return parts.astype(jnp.float32).sum(0).astype(jnp.bfloat16)]
    pallas_call x1, Pallas kernels: 6.78 us -> 5.8 us  [local(): pl.pallas_call(functools.partial(amplitudes, kdom, tile), in_specs=[smem,...]
where the time goes in v3:
time: 88.5 us; the launch traced here: 87.6 us
  blocking collectives  69.4 us (78%)
  Pallas kernels  8.73 us (10%)
  other arithmetic  3.17 us (4%)
  waiting for transfers between devices  2.4 us (3%)
  starting transfers between devices  1.92 us (2%)
  local copies, waits for them, and re-layouts  1.82 us (2%)
    all_to_all x2, blocking collectives, stage(): lax.all_to_all(tiles, ('grp', 'occ'), 0, 0, tiled=True, axis_index_groups...  41.3 us
    all_to_all x1, blocking collectives, local(): lax.all_to_all(blocks, 'occ', 0, 0, tiled=True, axis_index_groups=columns)  28.2 us
    pallas_call x1, Pallas kernels, local(): pl.pallas_call(functools.partial(amplitudes, kdom, tile), in_specs=[smem,...  5.8 us
    pallas_call x1, Pallas kernels, local(): pl.pallas_call(combine, in_specs=[smem, smem, vmem, vmem], out_specs=vmem...  2.93 us
    ppermute x1, waiting for transfers between devices, local(): got = lax.ppermute(sent, 'occ', [(i, i ^ 1) for i in range(nocc)])  2.4 us
    ppermute x1, starting transfers between devices, local(): got = lax.ppermute(sent, 'occ', [(i, i ^ 1) for i in range(nocc)])  1.92 us
    reduce_sum x2, other arithmetic, stage(): return parts.astype(jnp.float32).sum(0).astype(jnp.bfloat16)  1.82 us
  transfers between devices with their start and end apart: 1, of which 1 were waited for; matrix products, arithmetic and copies ran while one was open for 1% of the time, Pallas kernels for 0%

profile of v3, /device:TPU:6, one launch (start us, length us, event | category | flops | bytes accessed | tf_op | source)
XLA Modules:
  0.0 87.6 jit_solution(18077253278651901734)
XLA Ops:
  0.0 0.0 copy-start
  0.0 0.0 copy-start.1
  0.0 0.7 copy-done.1
  0.7 0.0 copy-start.2
  0.7 0.7 copy-done.2
  1.4 0.0 copy-start.3
  1.4 0.0 copy-start.4
  1.4 5.8 %amplitudes.1 = (bf16[48,128,128]{2,1,0:T(8,128)(2,1)S(1)}, bf16[48,128,128]{2,1,0:T(8,128)(2,1)}) custom-call(s32[1]{0:T(128)} %bitcast.me_ref, s32[256]{0:T(256)S(1)} %copy-done.2, bf16[8,768,256]{2,1,0:T(8,128)(2,1)} %b_hbm.1, bf16[8,768,128]{2,1,0:T(8,128)(2,1)} %q_hbm.1, f32[8,128]{1,0:T(8,128)S(1)} %copy-done.1), custom_call_target="tpu_custom_call" | custom-call | flops 805306368 | bytes 8388608 | tf_op jit(solution)/shard_map/amplitudes/pallas_call | solution.py:126
  7.2 1.9 %collective-permute-start = (bf16[48,128,128]{2,1,0:T(8,128)(2,1)}, bf16[48,128,128]{2,1,0:T(8,128)(2,1)S(1)}, u32[]{:S(2)}, u32[]{:S(2)}) collective-permute-start(bf16[48,128,128]{2,1,0:T(8,128)(2,1)} %get-tuple-element.8), channel_id=1, source_target_pairs={{0,1},{1,0},{2,3},{3,2},{4,5},{5,4},{6,7},{7,6},{8,9},{9,8},{10,11... | collective-permute-start | bytes 4718600 | tf_op jit(solution)/shard_map/ppermute | solution.py:145
  9.1 0.0 copy-done.3
  9.2 0.1 dynamic_slice.6
  9.2 0.0 copy-done
  9.2 0.1 constant_dynamic-slice_fusion
  9.3 0.0 copy-done.4
  9.3 0.2 select_reduce_fusion.1
  9.6 0.1 fusion.5
  9.7 0.1 add_select_fusion
  9.7 0.1 copy.12
  9.8 0.1 select_n.95
  9.9 0.2 fusion
  10.1 0.2 select_reduce_fusion.next_ref
  10.3 2.4 %collective-permute-done.got_ref = bf16[48,128,128]{2,1,0:T(8,128)(2,1)S(1)} collective-permute-done((bf16[48,128,128]{2,1,0:T(8,128)(2,1)}, bf16[48,128,128]{2,1,0:T(8,128)(2,1)S(1)}, u32[]{:S(2)}, u32[]{:S(2)}) %collective-permute-start) | collective-permute-done | bytes 1572896 | tf_op jit(solution)/shard_map/ppermute | solution.py:145
  12.7 2.9 %combine.1 = bf16[96,128,128]{2,1,0:T(8,128)(2,1)S(1)} custom-call(s32[96]{0:T(128)S(1)} %broadcast_select_fusion.1.slot_ref, s32[96]{0:T(128)S(1)} %select_reduce_fusion.next_ref, bf16[48,128,128]{2,1,0:T(8,128)(2,1)S(1)} %get-tuple-element.7.own_ref, bf16[48,128,128]{2,1,0:T(8,128)(2,1)S(1)} %collective-permute-done.got_ref), custom_call_target="tpu_custom_call" | custom-call | flops 4194304 | bytes 7340032 | tf_op jit(solution)/shard_map/combine/pallas_call | solution.py:166
  15.7 28.3 %all_to_all.15 = bf16[96,128,128]{2,1,0:T(8,128)(2,1)S(1)} all-to-all(bf16[96,128,128]{2,1,0:T(8,128)(2,1)S(1)} %combine.1), channel_id=1, replica_groups={{0,128,256,384},{32,160,288,416},{64,192,320,448},{96,224,352,480},{2,1..., dimensions={0} | all-to-all | bytes 6291456 | tf_op jit(solution)/shard_map/all_to_all | solution.py:182
  44.0 1.7 %reduce_sum.46 = bf16[24,128,128]{2,1,0:T(8,128)(2,1)} reduce(bf16[4,24,128,128]{3,2,1,0:T(8,128)(2,1)S(1)} %bitcast.7, bf16[]{:T(256)} %constant.72.clone.1), dimensions={0}, to_apply=%region_3.4 | reduce | flops 1179648 | bytes 3932162 | tf_op jit(solution)/shard_map/reduce_sum | solution.py:184
  45.7 12.9 %all_to_all.16 = bf16[24,128,128]{2,1,0:T(8,128)(2,1)S(1)} all-to-all(bf16[24,128,128]{2,1,0:T(8,128)(2,1)} %reduce_sum.46), channel_id=1, replica_groups={{0,32,64,96},{128,160,192,224},{256,288,320,352},{384,416,448,480},{2,3..., dimensions={0} | all-to-all | bytes 1572864 | tf_op jit(solution)/shard_map/all_to_all | solution.py:182
  58.6 0.1 reduce_sum.47
  58.8 28.2 %all_to_all.17 = bf16[16,6,8,128]{3,2,1,0:T(8,128)(2,1)S(1)} all-to-all(bf16[16,6,8,128]{3,2,1,0:T(8,128)(2,1)S(1)} %copy.13), channel_id=1, replica_groups={{0,2,4,6,8,10,12,14,16,18,20,22,24,26,28,30},{1,3,5,7,9,11,13,15,17,19,..., dimensions={0} | all-to-all | bytes 393216 | tf_op jit(solution)/shard_map/all_to_all | solution.py:191
  87.0 0.6 reduce_sum.48
  (4 shorter events, 0.1 us)
Async XLA Ops:
  0.0 9.2 %copy-start = (s32[256,6]{0,1:T(8,128)S(1)}, s32[256,6]{0,1:T(8,128)}, u32[]{:S(2)}) copy-start(s32[256,6]{0,1:T(8,128)} %param.9) | copy-start | bytes 18436
  0.0 0.7 copy-start.1
  0.7 0.7 copy-start.2
  1.4 7.8 %copy-start.3 = (s32[256]{0:T(256)S(1)}, s32[256]{0:T(256)}, u32[]{:S(2)}) copy-start(s32[256]{0:T(256)} %cnt_hbm.1) | copy-start | bytes 3076
  1.4 7.9 %copy-start.4 = (s32[96]{0:T(128)S(1)}, s32[96]{0:T(128)}, u32[]{:S(2)}) copy-start(s32[96]{0:T(128)} %param.11) | copy-start | bytes 1156
  7.2 5.5 %collective-permute-start = (bf16[48,128,128]{2,1,0:T(8,128)(2,1)}, bf16[48,128,128]{2,1,0:T(8,128)(2,1)S(1)}, u32[]{:S(2)}, u32[]{:S(2)}) collective-permute-start(bf16[48,128,128]{2,1,0:T(8,128)(2,1)} %get-tuple-element.8), channel_id=1, source_target_pairs={{0,1},{1,0},{2,3},{3,2},{4,5},{5,4},{6,7},{7,6},{8,9},{9,8},{10,11... | collective-permute-start | bytes 4718600 | tf_op jit(solution)/shard_map/ppermute | solution.py:145

commit v4 on v3

--- a/solution.py
+++ b/solution.py
@@ -46,14 +46,12 @@
         def part(tiles):
             rows = tiles * tile
             q = q_buf[i, :rows]
-            at = lax.broadcasted_iota(jnp.int32, q.shape, 0)
-            masked = jnp.where(at < used * tile, q.astype(jnp.float32), 0.0).astype(jnp.bfloat16)
-            h = lax.dot_general(b_buf[i, :rows], masked, (((0,), (0,)), ((), ())), preferred_element_type=jnp.float32)
+            h = lax.dot_general(b_buf[i, :rows], q, (((0,), (0,)), ((), ())), preferred_element_type=jnp.float32)
             h = h * row
             nb, nosv = h.shape
-            h = h.reshape(nb // (2 * LANES), 2, LANES, nosv)
-            even = h[:, 0].reshape(nb // 2, nosv)
-            odd = h[:, 1].reshape(nb // 2, nosv)
+            h = h.reshape(nb // (4 * LANES), 4, LANES, nosv)
+            even = jnp.concatenate([h[:, z].reshape(nb // 4, nosv) for z in (0, 2)], 0)
+            odd = jnp.concatenate([h[:, z].reshape(nb // 4, nosv) for z in (1, 3)], 0)
             scaled = jnp.concatenate([jnp.where(first, even, odd), jnp.where(first, odd, even)], 0)
             y = lax.dot_general(
                 scaled.astype(jnp.bfloat16), q, (((1,), (1,)), ((), ())), preferred_element_type=jnp.float32
@@ -62,10 +60,8 @@
                 keep_ref[i * kdom + k] = y[: nb // 2, k * tile : (k + 1) * tile]
                 send_ref[i * kdom + k] = y[nb // 2 :, k * tile : (k + 1) * tile]
 
-        for low in range(0, kdom, 2):
-            high = min(low + 2, kdom)
-            inside = used > low if high == kdom else jnp.logical_and(used > low, used <= high)
-            pl.when(inside)(functools.partial(part, high))
+        for tiles in range(1, kdom + 1):
+            pl.when(used == tiles)(functools.partial(part, tiles))
         store(i).start()
 
     @pl.loop(0, own)
@@ -73,40 +69,54 @@
         store(i).wait()
 
 
-def combine(slot_ref, next_ref, own_ref, got_ref, out_ref):
-    half = own_ref.shape[0]
-    tiles = 2 * half
+def place(each, heads, after, tiles_ref, out_ref, base):
+    count = tiles_ref.shape[0]
+    rows = out_ref.shape[1]
+
+    @pl.loop(0, count)
+    def _(t):
+        slot = heads[t]
+
+        @pl.when(slot >= 0)
+        def _():
+            at = slot // each * (2 * each) + slot % each
+            following = after[t]
+
+            def put(total):
+                out_ref[at] = total[:rows]
+                out_ref[at + each] = total[rows:]
+
+            def summed(total):
+                def body(state):
+                    n, total = state
+                    return after[n], total + tiles_ref[n].astype(jnp.float32)
+
+                total = total + tiles_ref[t].astype(jnp.float32)
+                put(lax.while_loop(lambda state: state[0] < count, body, (following, total))[1].astype(out_ref.dtype))
+
+            if base is None:
+                pl.when(following >= count)(lambda: put(tiles_ref[t]))
+                pl.when(following < count)(lambda: summed(0.0))
+            else:
+                summed(jnp.concatenate([base[at], base[at + each]], 0).astype(jnp.float32))
+
+
+def place_own(each, heads, after, own_ref, out_ref):
     out_ref[...] = jnp.zeros_like(out_ref)
-
-    def tile(t):
-        a = own_ref[jnp.minimum(t, half - 1)].astype(jnp.float32)
-        b = got_ref[jnp.maximum(t - half, 0)].astype(jnp.float32)
-        return jnp.where(t < half, a, b)
-
-    def enter(ref, offset):
-        @pl.loop(0, half)
-        def _(t):
-            slot = slot_ref[t + offset]
-
-            @pl.when(slot >= 0)
-            def _():
-                after = next_ref[t + offset]
-
-                @pl.when(after >= tiles)
-                def _():
-                    out_ref[slot] = ref[t]
-
-                @pl.when(after < tiles)
-                def _():
-                    def body(state):
-                        n, total = state
-                        return next_ref[n], total + tile(n)
-
-                    total = lax.while_loop(lambda state: state[0] < tiles, body, (after, ref[t].astype(jnp.float32)))[1]
-                    out_ref[slot] = total.astype(out_ref.dtype)
-
-    enter(own_ref, 0)
-    enter(got_ref, half)
+    place(each, heads, after, own_ref, out_ref, None)
+
+
+def place_got(each, heads, after, got_ref, base_ref, out_ref):
+    place(each, heads, after, got_ref, out_ref, out_ref)
+
+
+def add_parts(parts_ref, out_ref):
+    @pl.loop(0, out_ref.shape[0])
+    def _(t):
+        total = parts_ref[0, t].astype(jnp.float32)
+        for part in range(1, parts_ref.shape[0]):
+            total = total + parts_ref[part, t].astype(jnp.float32)
+        out_ref[t] = total.astype(out_ref.dtype)
 
 
 def local(ngrp, nocc, b_ints, osv_vecs, inv_denom, domains, dom_count, owner_slot):
@@ -155,41 +165,69 @@
     places = jnp.where(core == 0, owner_slot, turned)
     looked = jnp.sum(jnp.where(pair[:, :, None] == jnp.arange(ntiles, dtype=jnp.int32), places, 0), axis=-1)
     slots = jnp.where(keep, looked, -1)
-    slots = jnp.where(core == 0, slots, jnp.roll(slots, own, axis=0)).reshape(-1)
-    count = slots.shape[0]
-    order = jnp.arange(count, dtype=jnp.int32)
-    same = slots[:, None] == slots[None, :]
-    earlier = jnp.any(same & (order[None, :] < order[:, None]), axis=1)
+    slots = jnp.where(core == 0, slots, jnp.roll(slots, own, axis=0)).reshape(2, own * kdom)
+    order = jnp.arange(own * kdom, dtype=jnp.int32)
+    same = slots[:, :, None] == slots[:, None, :]
+    earlier = jnp.any(same & (order[None, :] < order[:, None]), axis=2)
     heads = jnp.where(earlier, -1, slots)
-    after = jnp.min(jnp.where(same & (order[None, :] > order[:, None]), order[None, :], count), axis=1)
-
+    after = jnp.min(jnp.where(same & (order[None, :] > order[:, None]), order[None, :], own * kdom), axis=2)
+
+    grid = jax.ShapeDtypeStruct((2 * ntiles, half // 2, tile), jnp.bfloat16)
     dense = pl.pallas_call(
-        combine,
+        functools.partial(place_own, each),
+        in_specs=[smem, smem, vmem],
+        out_specs=vmem,
+        out_shape=grid,
+        compiler_params=pltpu.CompilerParams(vmem_limit_bytes=24 << 20),
+        cost_estimate=pl.CostEstimate(flops=1 << 21, bytes_accessed=2 << 20, transcendentals=0),
+        name="place_own",
+    )(heads[0], after[0], kept)
+    dense = pl.pallas_call(
+        functools.partial(place_got, each),
         in_specs=[smem, smem, vmem, vmem],
         out_specs=vmem,
-        out_shape=jax.ShapeDtypeStruct((ntiles, half, tile), jnp.bfloat16),
+        out_shape=grid,
+        input_output_aliases={3: 0},
         compiler_params=pltpu.CompilerParams(vmem_limit_bytes=24 << 20),
-        cost_estimate=pl.CostEstimate(flops=1 << 22, bytes_accessed=7 << 20, transcendentals=0),
-        name="combine",
-    )(heads, after, kept, got)
+        name="place_got",
+    )(heads[1], after[1], got, dense)
+
+    nz = nocc // 2
 
     def line(along, fixed, z, c):
         chips = [(t, fixed) if along == 0 else (fixed, t) for t in range(side)]
         return [(x * side + y) * nocc + 2 * z + c for x, y in chips]
 
-    def stage(tiles, number):
-        groups = [line(number ^ c, fixed, z, c) for c in range(2) for z in range(nocc // 2) for fixed in range(side)]
-        parts = lax.all_to_all(tiles, ("grp", "occ"), 0, 0, tiled=True, axis_index_groups=groups)
-        parts = parts.reshape(side, tiles.shape[0] // side, half, tile)
-        return parts.astype(jnp.float32).sum(0).astype(jnp.bfloat16)
-
-    mine = stage(stage(dense, 0), 1)
-
-    nz = nocc // 2
-    columns = [[2 * z + c for z in range(nz)] for c in range(2)]
-    blocks = mine.reshape(ntiles // ngrp, nz, LANES, tile).transpose(1, 0, 2, 3)
-    parts = lax.all_to_all(blocks, "occ", 0, 0, tiled=True, axis_index_groups=columns)
-    return parts.astype(jnp.float32).sum(0).astype(jnp.bfloat16).transpose(1, 0, 2)
+    def summed(tiles, axes, groups):
+        parts = lax.all_to_all(tiles, axes, 0, 0, tiled=True, axis_index_groups=groups)
+        members = len(groups[0])
+        parts = parts.reshape(members, tiles.shape[0] // members, *tiles.shape[1:])
+        if parts.size < dense.size:
+            return parts.astype(jnp.float32).sum(0).astype(jnp.bfloat16)
+        return pl.pallas_call(
+            add_parts,
+            in_specs=[vmem],
+            out_specs=vmem,
+            out_shape=jax.ShapeDtypeStruct(parts.shape[1:], parts.dtype),
+            compiler_params=pltpu.CompilerParams(vmem_limit_bytes=24 << 20),
+            name="add_parts",
+        )(parts)
+
+    both = ("grp", "occ")
+    lines = [line(c, fixed, z, c) for c in range(2) for z in range(nz) for fixed in range(side)]
+    mine = summed(dense, both, lines)
+    planes = []
+    for c in range(2):
+        for z in range(0, nz, 2):
+            for fixed in range(side):
+                even = line(1 - c, fixed, z, c)
+                odd = line(1 - c, fixed, (z + 1 - 2 * c) % nz, c)
+                planes.append([device for pair in zip(even, odd) for device in pair])
+    mine = summed(mine, both, planes)
+    columns = [[2 * z + c for z in range(e, nz, 2)] for e in range(2) for c in range(2)]
+    blocks = mine.reshape(each, nz // 2, LANES, tile).transpose(1, 0, 2, 3)
+    blocks = blocks.reshape(nz // 2 * each, LANES, tile)
+    return summed(blocks, "occ", columns).transpose(1, 0, 2)
 
 
 def solution(mesh):

time: 88.5 us -> 85.2 us (0.963)
  waiting for transfers between devices: 2.4 us -> 0.01 us
  other arithmetic: 3.17 us -> 1.5 us
    ppermute x1, waiting for transfers between devices: 2.4 us -> 0.01 us  [local(): got = lax.ppermute(sent, 'occ', [(i, i ^ 1) for i in range(nocc)])]
    reduce_sum x3 -> x2, other arithmetic: 2.45 us -> 0.74 us  [summed(): return parts.astype(jnp.float32).sum(0).astype(jnp.bfloat16)]
    pallas_call x1 -> x3, Pallas kernels: 2.93 us -> 4.11 us  [the longest x1 1.88 us: local(): pl.pallas_call(functools.partial(place_own, each), in_specs=[smem, smem,...]
  transfers between devices with their start and end apart: 1 -> 1, of which waited for: 1 -> 0; matrix products, arithmetic and copies ran while one was open for 1% -> 2% of each run, Pallas kernels for 0% -> 2%
where the time goes in v4:
time: 85.2 us; the launch traced here: 84.3 us
  blocking collectives  68.7 us (81%)
  Pallas kernels  9.53 us (11%)
  local copies, waits for them, and re-layouts  2.37 us (3%)
  starting transfers between devices  2 us (2%)
  other arithmetic  1.5 us (2%)
    all_to_all x3, blocking collectives, summed(): lax.all_to_all(tiles, axes, 0, 0, tiled=True, axis_index_groups=groups)  68.7 us
    pallas_call x1, Pallas kernels, local(): pl.pallas_call(functools.partial(amplitudes, kdom, tile), in_specs=[smem,...  5.42 us
    ppermute x1, starting transfers between devices, local(): got = lax.ppermute(sent, 'occ', [(i, i ^ 1) for i in range(nocc)])  2 us
    pallas_call x1, Pallas kernels, local(): pl.pallas_call(functools.partial(place_own, each), in_specs=[smem, smem,...  1.88 us
  transfers between devices with their start and end apart: 1, of which 0 were waited for; matrix products, arithmetic and copies ran while one was open for 2% of the time, Pallas kernels for 2%

profile of v4, /device:TPU:6, one launch (start us, length us, event | category | flops | bytes accessed | tf_op | source)
XLA Modules:
  0.0 84.3 jit_solution(9582676935834519090)
XLA Ops:
  0.0 0.0 copy-start
  0.0 0.0 copy-start.3
  0.0 0.0 copy-start.4
  0.0 0.0 copy-start.1
  0.0 0.7 copy-done.1
  0.7 0.0 copy-start.2
  0.7 0.7 copy-done.2
  1.4 5.4 %amplitudes.1 = (bf16[48,128,128]{2,1,0:T(8,128)(2,1)S(1)}, bf16[48,128,128]{2,1,0:T(8,128)(2,1)}) custom-call(s32[1]{0:T(128)} %bitcast.2.me_ref, s32[256]{0:T(256)S(1)} %copy-done.2, bf16[8,768,256]{2,1,0:T(8,128)(2,1)} %b_hbm.1, bf16[8,768,128]{2,1,0:T(8,128)(2,1)} %q_hbm.1, f32[8,128]{1,0:T(8,128)S(1)} %copy-done.1), custom_call_target="tpu_custom_call" | custom-call | flops 805306368 | bytes 8388608 | tf_op jit(solution)/shard_map/amplitudes/pallas_call | solution.py:136
  6.8 2.0 %collective-permute-start = (bf16[48,128,128]{2,1,0:T(8,128)(2,1)}, bf16[48,128,128]{2,1,0:T(8,128)(2,1)S(1)}, u32[]{:S(2)}, u32[]{:S(2)}) collective-permute-start(bf16[48,128,128]{2,1,0:T(8,128)(2,1)} %get-tuple-element.7), channel_id=1, source_target_pairs={{0,1},{1,0},{2,3},{3,2},{4,5},{5,4},{6,7},{7,6},{8,9},{9,8},{10,11... | collective-permute-start | bytes 4718600 | tf_op jit(solution)/shard_map/ppermute | solution.py:155
  8.9 0.0 copy-done.3
  8.9 0.1 dynamic_slice.6
  8.9 0.0 copy-done
  8.9 0.1 constant_dynamic-slice_fusion
  9.0 0.0 copy-done.4
  9.0 0.2 select_reduce_fusion.1
  9.3 0.1 lt.90
  9.4 0.1 copy.12
  9.5 0.1 reduce_sum.36
  9.6 0.1 lt.100
  9.6 0.1 lt.87
  9.7 0.1 fusion.7
  9.8 0.1 pad_add_fusion
  9.9 0.1 copy.13
  10.0 0.1 concatenate.7
  10.0 0.1 lt.91
  10.1 0.1 lt.92
  10.3 0.2 fusion
  10.4 0.2 select_reduce_fusion
  10.7 1.9 %place_own.1.base_ref = bf16[192,64,128]{2,1,0:T(8,128)(2,1)S(1)} custom-call(s32[48]{0:T(128)S(1)} %get-tuple-element.18.heads, s32[48]{0:T(128)S(1)} %get-tuple-element.13.after, bf16[48,128,128]{2,1,0:T(8,128)(2,1)S(1)} %get-tuple-element.8.own_ref), custom_call_target="tpu_custom_call" | custom-call | flops 2097152 | bytes 2097152 | tf_op jit(solution)/shard_map/place_own/pallas_call | solution.py:176
  12.5 0.0 collective-permute-done.got_ref
  12.6 1.6 %place_got.1 = bf16[192,64,128]{2,1,0:T(8,128)(2,1)S(1)} custom-call(s32[48]{0:T(128)S(1)} %get-tuple-element.17.heads, s32[48]{0:T(128)S(1)} %get-tuple-element.14.after, bf16[48,128,128]{2,1,0:T(8,128)(2,1)S(1)} %collective-permute-done.got_ref, bf16[192,64,128]{2,1,0:T(8,128)(2,1)S(1)} %place_own.1.base_ref), custom_call_target="tpu_custom_call", output_to_operand_aliasing={{}: (3, {})} | custom-call | tf_op jit(solution)/shard_map/place_got/pallas_call | solution.py:185
  14.2 29.4 %all_to_all.15 = bf16[192,64,128]{2,1,0:T(8,128)(2,1)S(1)} all-to-all(bf16[192,64,128]{2,1,0:T(8,128)(2,1)S(1)} %place_got.1), channel_id=1, replica_groups={{0,128,256,384},{32,160,288,416},{64,192,320,448},{96,224,352,480},{2,1..., dimensions={0} | all-to-all | bytes 6291456 | tf_op jit(solution)/shard_map/all_to_all | solution.py:202
  43.5 0.6 add_parts.1
  44.2 12.5 %all_to_all.16 = bf16[48,64,128]{2,1,0:T(8,128)(2,1)S(1)} all-to-all(bf16[48,64,128]{2,1,0:T(8,128)(2,1)S(1)} %add_parts.1), channel_id=1, replica_groups={{0,2,32,34,64,66,96,98},{128,130,160,162,192,194,224,226},{256,258,288,..., dimensions={0} | all-to-all | bytes 1572864 | tf_op jit(solution)/shard_map/all_to_all | solution.py:202
  56.7 0.1 reduce_sum.37
  56.8 26.8 %all_to_all.17 = bf16[48,8,128]{2,1,0:T(8,128)(2,1)S(1)} all-to-all(bf16[48,8,128]{2,1,0:T(8,128)(2,1)S(1)} %bitcast.23), channel_id=1, replica_groups={{0,4,8,12,16,20,24,28},{1,5,9,13,17,21,25,29},{2,6,10,14,18,22,26,30},{..., dimensions={0} | all-to-all | bytes 196608 | tf_op jit(solution)/shard_map/all_to_all | solution.py:202
  83.7 0.6 reduce_sum.38
  (10 shorter events, 0.1 us)
Async XLA Ops:
  0.0 8.9 %copy-start = (s32[256,6]{0,1:T(8,128)S(1)}, s32[256,6]{0,1:T(8,128)}, u32[]{:S(2)}) copy-start(s32[256,6]{0,1:T(8,128)} %param.9) | copy-start | bytes 18436
  0.0 8.9 %copy-start.3 = (s32[256]{0:T(256)S(1)}, s32[256]{0:T(256)}, u32[]{:S(2)}) copy-start(s32[256]{0:T(256)} %cnt_hbm.1) | copy-start | bytes 3076
  0.0 9.0 %copy-start.4 = (s32[96]{0:T(128)S(1)}, s32[96]{0:T(128)}, u32[]{:S(2)}) copy-start(s32[96]{0:T(128)} %param.11) | copy-start | bytes 1156
  0.0 0.7 copy-start.1
  0.7 0.7 copy-start.2
  6.8 5.7 %collective-permute-start = (bf16[48,128,128]{2,1,0:T(8,128)(2,1)}, bf16[48,128,128]{2,1,0:T(8,128)(2,1)S(1)}, u32[]{:S(2)}, u32[]{:S(2)}) collective-permute-start(bf16[48,128,128]{2,1,0:T(8,128)(2,1)} %get-tuple-element.7), channel_id=1, source_target_pairs={{0,1},{1,0},{2,3},{3,2},{4,5},{5,4},{6,7},{7,6},{8,9},{9,8},{10,11... | collective-permute-start | bytes 4718600 | tf_op jit(solution)/shard_map/ppermute | solution.py:155

commit v5 on v4

--- a/solution.py
+++ b/solution.py
@@ -9,6 +9,7 @@
 from jax.sharding import PartitionSpec as P
 
 LANES = 8
+START = 5
 
 
 def amplitudes(kdom, tile, me_ref, cnt_hbm, b_hbm, q_hbm, inv_hbm, keep_ref, send_hbm, cnt, b_buf, q_buf, inv, send_ref, small, sems):
@@ -50,6 +51,7 @@
             h = h * row
             nb, nosv = h.shape
             h = h.reshape(nb // (4 * LANES), 4, LANES, nosv)
+            h = jnp.concatenate([h[START:], h[:START]], 0)
             even = jnp.concatenate([h[:, z].reshape(nb // 4, nosv) for z in (0, 2)], 0)
             odd = jnp.concatenate([h[:, z].reshape(nb // 4, nosv) for z in (1, 3)], 0)
             scaled = jnp.concatenate([jnp.where(first, even, odd), jnp.where(first, odd, even)], 0)
@@ -174,7 +176,7 @@
 
     grid = jax.ShapeDtypeStruct((2 * ntiles, half // 2, tile), jnp.bfloat16)
     dense = pl.pallas_call(
-        functools.partial(place_own, each),
+        functools.partial(place_own, side * each),
         in_specs=[smem, smem, vmem],
         out_specs=vmem,
         out_shape=grid,
@@ -183,7 +185,7 @@
         name="place_own",
     )(heads[0], after[0], kept)
     dense = pl.pallas_call(
-        functools.partial(place_got, each),
+        functools.partial(place_got, side * each),
         in_specs=[smem, smem, vmem, vmem],
         out_specs=vmem,
         out_shape=grid,
@@ -222,9 +224,10 @@
             for fixed in range(side):
                 even = line(1 - c, fixed, z, c)
                 odd = line(1 - c, fixed, (z + 1 - 2 * c) % nz, c)
-                planes.append([device for pair in zip(even, odd) for device in pair])
+                planes.append(even + odd)
     mine = summed(mine, both, planes)
-    columns = [[2 * z + c for z in range(e, nz, 2)] for e in range(2) for c in range(2)]
+    order = [(z + START) % (nz // 2) for z in range(nz // 2)]
+    columns = [[2 * (2 * z + e) + c for z in order] for e in range(2) for c in range(2)]
     blocks = mine.reshape(each, nz // 2, LANES, tile).transpose(1, 0, 2, 3)
     blocks = blocks.reshape(nz // 2 * each, LANES, tile)
     return summed(blocks, "occ", columns).transpose(1, 0, 2)

time: 85.2 us -> 79.8 us (0.937)
  blocking collectives: 68.7 us -> 62.7 us
    all_to_all x3, blocking collectives: 68.7 us -> 62.7 us  [summed(): lax.all_to_all(tiles, axes, 0, 0, tiled=True, axis_index_groups=groups)]
  transfers between devices with their start and end apart: 1 -> 1, of which waited for: 0 -> 0; matrix products, arithmetic and copies ran while one was open for 2% -> 2% of each run, Pallas kernels for 2% -> 3%
where the time goes in v5:
time: 79.8 us; the launch traced here: 78.6 us
  blocking collectives  62.7 us (79%)
  Pallas kernels  9.97 us (12%)
  local copies, waits for them, and re-layouts  2.37 us (3%)
  starting transfers between devices  1.92 us (2%)
  other arithmetic  1.5 us (2%)
    all_to_all x3, blocking collectives, summed(): lax.all_to_all(tiles, axes, 0, 0, tiled=True, axis_index_groups=groups)  62.7 us
    pallas_call x1, Pallas kernels, local(): pl.pallas_call(functools.partial(amplitudes, kdom, tile), in_specs=[smem,...  5.7 us
    pallas_call x1, Pallas kernels, local(): pl.pallas_call(functools.partial(place_own, side * each), in_specs=[smem,...  1.98 us
    ppermute x1, starting transfers between devices, local(): got = lax.ppermute(sent, 'occ', [(i, i ^ 1) for i in range(nocc)])  1.92 us
    pallas_call x1, Pallas kernels, local(): pl.pallas_call(functools.partial(place_got, side * each), in_specs=[smem,...  1.66 us
  transfers between devices with their start and end apart: 1, of which 0 were waited for; matrix products, arithmetic and copies ran while one was open for 2% of the time, Pallas kernels for 3%

profile of v5, /device:TPU:6, one launch (start us, length us, event | category | flops | bytes accessed | tf_op | source)
XLA Modules:
  0.0 78.6 jit_solution(6691732746622077543)
XLA Ops:
  0.0 0.0 copy-start
  0.0 0.0 copy-start.3
  0.0 0.0 copy-start.4
  0.0 0.0 copy-start.1
  0.0 0.7 copy-done.1
  0.7 0.0 copy-start.2
  0.7 0.7 copy-done.2
  1.4 5.7 %amplitudes.1 = (bf16[48,128,128]{2,1,0:T(8,128)(2,1)S(1)}, bf16[48,128,128]{2,1,0:T(8,128)(2,1)}) custom-call(s32[1]{0:T(128)} %bitcast.2.me_ref, s32[256]{0:T(256)S(1)} %copy-done.2, bf16[8,768,256]{2,1,0:T(8,128)(2,1)} %b_hbm.1, bf16[8,768,128]{2,1,0:T(8,128)(2,1)} %q_hbm.1, f32[8,128]{1,0:T(8,128)S(1)} %copy-done.1), custom_call_target="tpu_custom_call" | custom-call | flops 805306368 | bytes 8388608 | tf_op jit(solution)/shard_map/amplitudes/pallas_call | solution.py:138
  7.1 1.9 %collective-permute-start = (bf16[48,128,128]{2,1,0:T(8,128)(2,1)}, bf16[48,128,128]{2,1,0:T(8,128)(2,1)S(1)}, u32[]{:S(2)}, u32[]{:S(2)}) collective-permute-start(bf16[48,128,128]{2,1,0:T(8,128)(2,1)} %get-tuple-element.7), channel_id=1, source_target_pairs={{0,1},{1,0},{2,3},{3,2},{4,5},{5,4},{6,7},{7,6},{8,9},{9,8},{10,11... | collective-permute-start | bytes 4718600 | tf_op jit(solution)/shard_map/ppermute | solution.py:157
  9.1 0.0 copy-done.3
  9.1 0.1 dynamic_slice.6
  9.1 0.0 copy-done
  9.1 0.1 constant_dynamic-slice_fusion
  9.2 0.0 copy-done.4
  9.2 0.2 select_reduce_fusion.1
  9.5 0.1 lt.90
  9.6 0.1 copy.12
  9.7 0.1 reduce_sum.36
  9.8 0.1 lt.100
  9.8 0.1 lt.87
  9.9 0.1 fusion.7
  10.0 0.1 pad_add_fusion
  10.1 0.1 copy.13
  10.2 0.1 concatenate.7
  10.3 0.1 lt.91
  10.3 0.1 lt.92
  10.5 0.2 fusion
  10.6 0.2 select_reduce_fusion
  10.9 2.0 %place_own.1.base_ref = bf16[192,64,128]{2,1,0:T(8,128)(2,1)S(1)} custom-call(s32[48]{0:T(128)S(1)} %get-tuple-element.18.heads, s32[48]{0:T(128)S(1)} %get-tuple-element.13.after, bf16[48,128,128]{2,1,0:T(8,128)(2,1)S(1)} %get-tuple-element.8.own_ref), custom_call_target="tpu_custom_call" | custom-call | flops 2097152 | bytes 2097152 | tf_op jit(solution)/shard_map/place_own/pallas_call | solution.py:178
  12.8 0.0 collective-permute-done.got_ref
  12.9 1.7 %place_got.1 = bf16[192,64,128]{2,1,0:T(8,128)(2,1)S(1)} custom-call(s32[48]{0:T(128)S(1)} %get-tuple-element.17.heads, s32[48]{0:T(128)S(1)} %get-tuple-element.14.after, bf16[48,128,128]{2,1,0:T(8,128)(2,1)S(1)} %collective-permute-done.got_ref, bf16[192,64,128]{2,1,0:T(8,128)(2,1)S(1)} %place_own.1.base_ref), custom_call_target="tpu_custom_call", output_to_operand_aliasing={{}: (3, {})} | custom-call | tf_op jit(solution)/shard_map/place_got/pallas_call | solution.py:187
  14.5 28.2 %all_to_all.15 = bf16[192,64,128]{2,1,0:T(8,128)(2,1)S(1)} all-to-all(bf16[192,64,128]{2,1,0:T(8,128)(2,1)S(1)} %place_got.1), channel_id=1, replica_groups={{0,128,256,384},{32,160,288,416},{64,192,320,448},{96,224,352,480},{2,1..., dimensions={0} | all-to-all | bytes 6291456 | tf_op jit(solution)/shard_map/all_to_all | solution.py:204
  42.7 0.6 add_parts.1
  43.3 12.5 %all_to_all.16 = bf16[48,64,128]{2,1,0:T(8,128)(2,1)S(1)} all-to-all(bf16[48,64,128]{2,1,0:T(8,128)(2,1)S(1)} %add_parts.1), channel_id=1, replica_groups={{0,32,64,96,2,34,66,98},{128,160,192,224,130,162,194,226},{256,288,320,..., dimensions={0} | all-to-all | bytes 1572864 | tf_op jit(solution)/shard_map/all_to_all | solution.py:204
  55.8 0.1 reduce_sum.37
  56.0 22.0 %all_to_all.17 = bf16[48,8,128]{2,1,0:T(8,128)(2,1)S(1)} all-to-all(bf16[48,8,128]{2,1,0:T(8,128)(2,1)S(1)} %bitcast.23), channel_id=1, replica_groups={{20,24,28,0,4,8,12,16},{21,25,29,1,5,9,13,17},{22,26,30,2,6,10,14,18},{..., dimensions={0} | all-to-all | bytes 196608 | tf_op jit(solution)/shard_map/all_to_all | solution.py:204
  78.0 0.6 reduce_sum.38
  (10 shorter events, 0.1 us)
Async XLA Ops:
  0.0 9.1 %copy-start = (s32[256,6]{0,1:T(8,128)S(1)}, s32[256,6]{0,1:T(8,128)}, u32[]{:S(2)}) copy-start(s32[256,6]{0,1:T(8,128)} %param.9) | copy-start | bytes 18436
  0.0 9.1 %copy-start.3 = (s32[256]{0:T(256)S(1)}, s32[256]{0:T(256)}, u32[]{:S(2)}) copy-start(s32[256]{0:T(256)} %cnt_hbm.1) | copy-start | bytes 3076
  0.0 9.2 %copy-start.4 = (s32[96]{0:T(128)S(1)}, s32[96]{0:T(128)}, u32[]{:S(2)}) copy-start(s32[96]{0:T(128)} %param.11) | copy-start | bytes 1156
  0.0 0.7 copy-start.1
  0.7 0.7 copy-start.2
  7.1 5.7 %collective-permute-start = (bf16[48,128,128]{2,1,0:T(8,128)(2,1)}, bf16[48,128,128]{2,1,0:T(8,128)(2,1)S(1)}, u32[]{:S(2)}, u32[]{:S(2)}) collective-permute-start(bf16[48,128,128]{2,1,0:T(8,128)(2,1)} %get-tuple-element.7), channel_id=1, source_target_pairs={{0,1},{1,0},{2,3},{3,2},{4,5},{5,4},{6,7},{7,6},{8,9},{9,8},{10,11... | collective-permute-start | bytes 4718600 | tf_op jit(solution)/shard_map/ppermute | solution.py:157

commit v6 on v5

--- a/solution.py
+++ b/solution.py
@@ -9,6 +9,7 @@
 from jax.sharding import PartitionSpec as P
 
 LANES = 8
+TURN = 2
 START = 5
 
 
@@ -163,8 +164,9 @@
     side = math.isqrt(ngrp)
     each = ntiles // ngrp
     owner, within = owner_slot // each, owner_slot % each
-    turned = ((owner % side) * side + owner // side) * each + within
-    places = jnp.where(core == 0, owner_slot, turned)
+    along_x, along_y = (owner // side - TURN) % side, (owner % side - TURN) % side
+    first, second = jnp.where(core == 0, along_x, along_y), jnp.where(core == 0, along_y, along_x)
+    places = (first * side + second) * each + within
     looked = jnp.sum(jnp.where(pair[:, :, None] == jnp.arange(ntiles, dtype=jnp.int32), places, 0), axis=-1)
     slots = jnp.where(keep, looked, -1)
     slots = jnp.where(core == 0, slots, jnp.roll(slots, own, axis=0)).reshape(2, own * kdom)
@@ -195,9 +197,10 @@
     )(heads[1], after[1], got, dense)
 
     nz = nocc // 2
+    turned = [(t + TURN) % side for t in range(side)]
 
     def line(along, fixed, z, c):
-        chips = [(t, fixed) if along == 0 else (fixed, t) for t in range(side)]
+        chips = [(t, fixed) if along == 0 else (fixed, t) for t in turned]
         return [(x * side + y) * nocc + 2 * z + c for x, y in chips]
 
     def summed(tiles, axes, groups):

time: 79.8 us -> 79 us (0.990)
  the two profiles are of different devices: /device:TPU:6 before, /device:TPU:1 now
where the time goes in v6:
time: 79 us; the launch traced here: 78.7 us
  blocking collectives  55.7 us (71%)
  Pallas kernels  10.2 us (13%)
  starting transfers between devices  8.66 us (11%)
  local copies, waits for them, and re-layouts  2.37 us (3%)
  other arithmetic  1.51 us (2%)
    all_to_all x3, blocking collectives, summed(): lax.all_to_all(tiles, axes, 0, 0, tiled=True, axis_index_groups=groups)  55.7 us
    ppermute x1, starting transfers between devices, local(): got = lax.ppermute(sent, 'occ', [(i, i ^ 1) for i in range(nocc)])  8.66 us
    pallas_call x1, Pallas kernels, local(): pl.pallas_call(functools.partial(amplitudes, kdom, tile), in_specs=[smem,...  5.96 us
    pallas_call x1, Pallas kernels, local(): pl.pallas_call(functools.partial(place_own, side * each), in_specs=[smem,...  2.02 us
    pallas_call x1, Pallas kernels, local(): pl.pallas_call(functools.partial(place_got, side * each), in_specs=[smem,...  1.63 us
  transfers between devices with their start and end apart: 1, of which 0 were waited for; matrix products, arithmetic and copies ran while one was open for 2% of the time, Pallas kernels for 3%

profile of v6, /device:TPU:1, one launch (start us, length us, event | category | flops | bytes accessed | tf_op | source)
XLA Modules:
  0.0 78.7 jit_solution(633973697961542241)
XLA Ops:
  0.0 0.0 copy-start
  0.0 0.0 copy-start.3
  0.0 0.0 copy-start.4
  0.0 0.0 copy-start.1
  0.0 0.7 copy-done.1
  0.7 0.0 copy-start.2
  0.7 0.7 copy-done.2
  1.4 6.0 %amplitudes.1 = (bf16[48,128,128]{2,1,0:T(8,128)(2,1)S(1)}, bf16[48,128,128]{2,1,0:T(8,128)(2,1)}) custom-call(s32[1]{0:T(128)} %bitcast.2.me_ref, s32[256]{0:T(256)S(1)} %copy-done.2, bf16[8,768,256]{2,1,0:T(8,128)(2,1)} %b_hbm.1, bf16[8,768,128]{2,1,0:T(8,128)(2,1)} %q_hbm.1, f32[8,128]{1,0:T(8,128)S(1)} %copy-done.1), custom_call_target="tpu_custom_call" | custom-call | flops 805306368 | bytes 8388608 | tf_op jit(solution)/shard_map/amplitudes/pallas_call | solution.py:139
  7.4 8.7 %collective-permute-start = (bf16[48,128,128]{2,1,0:T(8,128)(2,1)}, bf16[48,128,128]{2,1,0:T(8,128)(2,1)S(1)}, u32[]{:S(2)}, u32[]{:S(2)}) collective-permute-start(bf16[48,128,128]{2,1,0:T(8,128)(2,1)} %get-tuple-element.7), channel_id=1, source_target_pairs={{0,1},{1,0},{2,3},{3,2},{4,5},{5,4},{6,7},{7,6},{8,9},{9,8},{10,11... | collective-permute-start | bytes 4718600 | tf_op jit(solution)/shard_map/ppermute | solution.py:158
  16.1 0.0 copy-done.3
  16.1 0.1 dynamic_slice.6
  16.1 0.0 copy-done
  16.1 0.1 constant_dynamic-slice_fusion
  16.2 0.0 copy-done.4
  16.3 0.2 select_reduce_fusion.1
  16.5 0.1 lt.98
  16.6 0.1 copy.12
  16.7 0.1 reduce_sum.36
  16.8 0.1 lt.110
  16.9 0.1 lt.95
  16.9 0.1 fusion.10
  17.0 0.1 pad_add_fusion
  17.1 0.1 copy.13
  17.2 0.1 concatenate.7
  17.3 0.1 lt.99
  17.3 0.1 lt.100
  17.5 0.2 fusion
  17.6 0.2 select_reduce_fusion
  17.9 2.0 %place_own.1.base_ref = bf16[192,64,128]{2,1,0:T(8,128)(2,1)S(1)} custom-call(s32[48]{0:T(128)S(1)} %get-tuple-element.18.heads, s32[48]{0:T(128)S(1)} %get-tuple-element.13.after, bf16[48,128,128]{2,1,0:T(8,128)(2,1)S(1)} %get-tuple-element.8.own_ref), custom_call_target="tpu_custom_call" | custom-call | flops 2097152 | bytes 2097152 | tf_op jit(solution)/shard_map/place_own/pallas_call | solution.py:180
  19.9 0.0 collective-permute-done.got_ref
  19.9 1.6 %place_got.1 = bf16[192,64,128]{2,1,0:T(8,128)(2,1)S(1)} custom-call(s32[48]{0:T(128)S(1)} %get-tuple-element.17.heads, s32[48]{0:T(128)S(1)} %get-tuple-element.14.after, bf16[48,128,128]{2,1,0:T(8,128)(2,1)S(1)} %collective-permute-done.got_ref, bf16[192,64,128]{2,1,0:T(8,128)(2,1)S(1)} %place_own.1.base_ref), custom_call_target="tpu_custom_call", output_to_operand_aliasing={{}: (3, {})} | custom-call | tf_op jit(solution)/shard_map/place_got/pallas_call | solution.py:189
  21.5 22.6 %all_to_all.15 = bf16[192,64,128]{2,1,0:T(8,128)(2,1)S(1)} all-to-all(bf16[192,64,128]{2,1,0:T(8,128)(2,1)S(1)} %place_got.1), channel_id=1, replica_groups={{256,384,0,128},{288,416,32,160},{320,448,64,192},{352,480,96,224},{258..., dimensions={0} | all-to-all | bytes 6291456 | tf_op jit(solution)/shard_map/all_to_all | solution.py:207
  44.2 0.6 add_parts.1
  44.8 17.4 %all_to_all.16 = bf16[48,64,128]{2,1,0:T(8,128)(2,1)S(1)} all-to-all(bf16[48,64,128]{2,1,0:T(8,128)(2,1)S(1)} %add_parts.1), channel_id=1, replica_groups={{64,96,0,32,66,98,2,34},{192,224,128,160,194,226,130,162},{320,352,256,..., dimensions={0} | all-to-all | bytes 1572864 | tf_op jit(solution)/shard_map/all_to_all | solution.py:207
  62.2 0.1 reduce_sum.37
  62.4 15.7 %all_to_all.17 = bf16[48,8,128]{2,1,0:T(8,128)(2,1)S(1)} all-to-all(bf16[48,8,128]{2,1,0:T(8,128)(2,1)S(1)} %bitcast.23), channel_id=1, replica_groups={{20,24,28,0,4,8,12,16},{21,25,29,1,5,9,13,17},{22,26,30,2,6,10,14,18},{..., dimensions={0} | all-to-all | bytes 196608 | tf_op jit(solution)/shard_map/all_to_all | solution.py:207
  78.1 0.6 reduce_sum.38
  (10 shorter events, 0.1 us)
Async XLA Ops:
  0.0 16.1 %copy-start = (s32[256,6]{0,1:T(8,128)S(1)}, s32[256,6]{0,1:T(8,128)}, u32[]{:S(2)}) copy-start(s32[256,6]{0,1:T(8,128)} %param.9) | copy-start | bytes 18436
  0.0 16.1 %copy-start.3 = (s32[256]{0:T(256)S(1)}, s32[256]{0:T(256)}, u32[]{:S(2)}) copy-start(s32[256]{0:T(256)} %cnt_hbm.1) | copy-start | bytes 3076
  0.0 16.2 %copy-start.4 = (s32[96]{0:T(128)S(1)}, s32[96]{0:T(128)}, u32[]{:S(2)}) copy-start(s32[96]{0:T(128)} %param.11) | copy-start | bytes 1156
  0.0 0.7 copy-start.1
  0.7 0.7 copy-start.2
  7.4 12.5 %collective-permute-start = (bf16[48,128,128]{2,1,0:T(8,128)(2,1)}, bf16[48,128,128]{2,1,0:T(8,128)(2,1)S(1)}, u32[]{:S(2)}, u32[]{:S(2)}) collective-permute-start(bf16[48,128,128]{2,1,0:T(8,128)(2,1)} %get-tuple-element.7), channel_id=1, source_target_pairs={{0,1},{1,0},{2,3},{3,2},{4,5},{5,4},{6,7},{7,6},{8,9},{9,8},{10,11... | collective-permute-start | bytes 4718600 | tf_op jit(solution)/shard_map/ppermute | solution.py:158

commit v7 on v6

--- a/solution.py
+++ b/solution.py
@@ -13,7 +13,7 @@
 START = 5
 
 
-def amplitudes(kdom, tile, me_ref, cnt_hbm, b_hbm, q_hbm, inv_hbm, keep_ref, send_hbm, cnt, b_buf, q_buf, inv, send_ref, small, sems):
+def amplitudes(kdom, tile, me_ref, cnt_hbm, b_hbm, q_hbm, inv_hbm, keep_ref, send_hbm, cnt, b_buf, q_buf, inv, scaled, send_ref, small, sems):
     own = b_buf.shape[0]
     me = me_ref[0]
     counts = pltpu.make_async_copy(cnt_hbm, cnt, small.at[0])
@@ -38,34 +38,33 @@
     gaps.wait()
     first = me % 2 == 0
 
-    @pl.loop(0, own)
-    def _(i):
+    def contract(i):
         for copy in fetch(i):
             copy.wait()
-        used = cnt[me * own + i]
-        row = inv[pl.ds(i, 1), :]
-
-        def part(tiles):
-            rows = tiles * tile
-            q = q_buf[i, :rows]
-            h = lax.dot_general(b_buf[i, :rows], q, (((0,), (0,)), ((), ())), preferred_element_type=jnp.float32)
-            h = h * row
-            nb, nosv = h.shape
-            h = h.reshape(nb // (4 * LANES), 4, LANES, nosv)
-            h = jnp.concatenate([h[START:], h[:START]], 0)
-            even = jnp.concatenate([h[:, z].reshape(nb // 4, nosv) for z in (0, 2)], 0)
-            odd = jnp.concatenate([h[:, z].reshape(nb // 4, nosv) for z in (1, 3)], 0)
-            scaled = jnp.concatenate([jnp.where(first, even, odd), jnp.where(first, odd, even)], 0)
-            y = lax.dot_general(
-                scaled.astype(jnp.bfloat16), q, (((1,), (1,)), ((), ())), preferred_element_type=jnp.float32
-            ).astype(jnp.bfloat16)
-            for k in range(tiles):
-                keep_ref[i * kdom + k] = y[: nb // 2, k * tile : (k + 1) * tile]
-                send_ref[i * kdom + k] = y[nb // 2 :, k * tile : (k + 1) * tile]
-
-        for tiles in range(1, kdom + 1):
-            pl.when(used == tiles)(functools.partial(part, tiles))
+        q = q_buf[i]
+        at = lax.broadcasted_iota(jnp.int32, q.shape, 0)
+        used = cnt[me * own + i] * tile
+        q = jnp.where(at < used, q.astype(jnp.float32), 0.0).astype(jnp.bfloat16)
+        h = lax.dot_general(b_buf[i], q, (((0,), (0,)), ((), ())), preferred_element_type=jnp.float32)
+        h = h * inv[pl.ds(i, 1), :]
+        nb, nosv = h.shape
+        h = h.reshape(nb // (4 * LANES), 4, LANES, nosv)
+        h = jnp.concatenate([h[START:], h[:START]], 0)
+        even = jnp.concatenate([h[:, z].reshape(nb // 4, nosv) for z in (0, 2)], 0)
+        odd = jnp.concatenate([h[:, z].reshape(nb // 4, nosv) for z in (1, 3)], 0)
+        scaled[i] = jnp.concatenate([jnp.where(first, even, odd), jnp.where(first, odd, even)], 0).astype(scaled.dtype)
+
+    def expand(i):
+        half = scaled.shape[1] // 2
+        y = lax.dot_general(scaled[i], q_buf[i], (((1,), (1,)), ((), ())), preferred_element_type=jnp.float32)
+        y = y.astype(jnp.bfloat16)
+        for k in range(kdom):
+            keep_ref[i * kdom + k] = y[:half, k * tile : (k + 1) * tile]
+            send_ref[i * kdom + k] = y[half:, k * tile : (k + 1) * tile]
         store(i).start()
+
+    pl.loop(0, own, unroll=own)(contract)
+    pl.loop(0, own, unroll=own)(expand)
 
     @pl.loop(0, own)
     def _(i):
@@ -146,6 +145,7 @@
             pltpu.VMEM(b_ints.shape, b_ints.dtype),
             pltpu.VMEM(osv_vecs.shape, osv_vecs.dtype),
             pltpu.VMEM(inv_denom.shape, inv_denom.dtype),
+            pltpu.VMEM((own, nb, nosv), jnp.bfloat16),
             pltpu.VMEM(half_tiles.shape, half_tiles.dtype),
             pltpu.SemaphoreType.DMA((2,)),
             pltpu.SemaphoreType.DMA((3, own)),

time: 79 us -> 77.8 us (0.985)
  the two profiles are of different devices: /device:TPU:1 before, /device:TPU:6 now
where the time goes in v7:
time: 77.8 us; the launch traced here: 76.6 us
  blocking collectives  60.8 us (78%)
  Pallas kernels  9.83 us (13%)
  local copies, waits for them, and re-layouts  2.37 us (3%)
  starting transfers between devices  1.92 us (2%)
  other arithmetic  1.51 us (2%)
    all_to_all x3, blocking collectives, summed(): lax.all_to_all(tiles, axes, 0, 0, tiled=True, axis_index_groups=groups)  60.8 us
    pallas_call x1, Pallas kernels, local(): pl.pallas_call(functools.partial(amplitudes, kdom, tile), in_specs=[smem,...  5.46 us
    pallas_call x1, Pallas kernels, local(): pl.pallas_call(functools.partial(place_own, side * each), in_specs=[smem,...  2.03 us
    ppermute x1, starting transfers between devices, local(): got = lax.ppermute(sent, 'occ', [(i, i ^ 1) for i in range(nocc)])  1.92 us
    pallas_call x1, Pallas kernels, local(): pl.pallas_call(functools.partial(place_got, side * each), in_specs=[smem,...  1.71 us
  transfers between devices with their start and end apart: 1, of which 0 were waited for; matrix products, arithmetic and copies ran while one was open for 2% of the time, Pallas kernels for 3%

profile of v7, /device:TPU:6, one launch (start us, length us, event | category | flops | bytes accessed | tf_op | source)
XLA Modules:
  0.0 76.6 jit_solution(13877324114778806740)
XLA Ops:
  0.0 0.0 copy-start
  0.0 0.0 copy-start.3
  0.0 0.0 copy-start.4
  0.0 0.0 copy-start.1
  0.0 0.7 copy-done.1
  0.7 0.0 copy-start.2
  0.7 0.7 copy-done.2
  1.4 5.5 %amplitudes.1 = (bf16[48,128,128]{2,1,0:T(8,128)(2,1)S(1)}, bf16[48,128,128]{2,1,0:T(8,128)(2,1)}) custom-call(s32[1]{0:T(128)} %bitcast.2.me_ref, s32[256]{0:T(256)S(1)} %copy-done.2, bf16[8,768,256]{2,1,0:T(8,128)(2,1)} %b_hbm.1, bf16[8,768,128]{2,1,0:T(8,128)(2,1)} %q_hbm.1, f32[8,128]{1,0:T(8,128)S(1)} %copy-done.1), custom_call_target="tpu_custom_call" | custom-call | flops 805306368 | bytes 8388608 | tf_op jit(solution)/shard_map/amplitudes/pallas_call | solution.py:138
  6.9 1.9 %collective-permute-start = (bf16[48,128,128]{2,1,0:T(8,128)(2,1)}, bf16[48,128,128]{2,1,0:T(8,128)(2,1)S(1)}, u32[]{:S(2)}, u32[]{:S(2)}) collective-permute-start(bf16[48,128,128]{2,1,0:T(8,128)(2,1)} %get-tuple-element.7), channel_id=1, source_target_pairs={{0,1},{1,0},{2,3},{3,2},{4,5},{5,4},{6,7},{7,6},{8,9},{9,8},{10,11... | collective-permute-start | bytes 4718600 | tf_op jit(solution)/shard_map/ppermute | solution.py:158
  8.8 0.0 copy-done.3
  8.8 0.1 dynamic_slice.6
  8.9 0.0 copy-done
  8.9 0.1 constant_dynamic-slice_fusion
  9.0 0.0 copy-done.4
  9.0 0.2 select_reduce_fusion.1
  9.3 0.1 lt.98
  9.4 0.1 copy.12
  9.4 0.1 reduce_sum.36
  9.5 0.1 lt.110
  9.6 0.1 lt.95
  9.7 0.1 fusion.10
  9.8 0.1 pad_add_fusion
  9.8 0.1 copy.13
  9.9 0.1 concatenate.7
  10.0 0.1 lt.99
  10.1 0.1 lt.100
  10.2 0.2 fusion
  10.4 0.2 select_reduce_fusion
  10.6 2.0 %place_own.1.base_ref = bf16[192,64,128]{2,1,0:T(8,128)(2,1)S(1)} custom-call(s32[48]{0:T(128)S(1)} %get-tuple-element.18.heads, s32[48]{0:T(128)S(1)} %get-tuple-element.13.after, bf16[48,128,128]{2,1,0:T(8,128)(2,1)S(1)} %get-tuple-element.8.own_ref), custom_call_target="tpu_custom_call" | custom-call | flops 2097152 | bytes 2097152 | tf_op jit(solution)/shard_map/place_own/pallas_call | solution.py:180
  12.7 0.0 collective-permute-done.got_ref
  12.7 1.7 %place_got.1 = bf16[192,64,128]{2,1,0:T(8,128)(2,1)S(1)} custom-call(s32[48]{0:T(128)S(1)} %get-tuple-element.17.heads, s32[48]{0:T(128)S(1)} %get-tuple-element.14.after, bf16[48,128,128]{2,1,0:T(8,128)(2,1)S(1)} %collective-permute-done.got_ref, bf16[192,64,128]{2,1,0:T(8,128)(2,1)S(1)} %place_own.1.base_ref), custom_call_target="tpu_custom_call", output_to_operand_aliasing={{}: (3, {})} | custom-call | tf_op jit(solution)/shard_map/place_got/pallas_call | solution.py:189
  14.4 29.0 %all_to_all.15 = bf16[192,64,128]{2,1,0:T(8,128)(2,1)S(1)} all-to-all(bf16[192,64,128]{2,1,0:T(8,128)(2,1)S(1)} %place_got.1), channel_id=1, replica_groups={{256,384,0,128},{288,416,32,160},{320,448,64,192},{352,480,96,224},{258..., dimensions={0} | all-to-all | bytes 6291456 | tf_op jit(solution)/shard_map/all_to_all | solution.py:207
  43.4 0.6 add_parts.1
  44.1 12.0 %all_to_all.16 = bf16[48,64,128]{2,1,0:T(8,128)(2,1)S(1)} all-to-all(bf16[48,64,128]{2,1,0:T(8,128)(2,1)S(1)} %add_parts.1), channel_id=1, replica_groups={{64,96,0,32,66,98,2,34},{192,224,128,160,194,226,130,162},{320,352,256,..., dimensions={0} | all-to-all | bytes 1572864 | tf_op jit(solution)/shard_map/all_to_all | solution.py:207
  56.1 0.1 reduce_sum.37
  56.2 19.7 %all_to_all.17 = bf16[48,8,128]{2,1,0:T(8,128)(2,1)S(1)} all-to-all(bf16[48,8,128]{2,1,0:T(8,128)(2,1)S(1)} %bitcast.23), channel_id=1, replica_groups={{20,24,28,0,4,8,12,16},{21,25,29,1,5,9,13,17},{22,26,30,2,6,10,14,18},{..., dimensions={0} | all-to-all | bytes 196608 | tf_op jit(solution)/shard_map/all_to_all | solution.py:207
  76.0 0.6 reduce_sum.38
  (10 shorter events, 0.1 us)
Async XLA Ops:
  0.0 8.9 %copy-start = (s32[256,6]{0,1:T(8,128)S(1)}, s32[256,6]{0,1:T(8,128)}, u32[]{:S(2)}) copy-start(s32[256,6]{0,1:T(8,128)} %param.9) | copy-start | bytes 18436
  0.0 8.8 %copy-start.3 = (s32[256]{0:T(256)S(1)}, s32[256]{0:T(256)}, u32[]{:S(2)}) copy-start(s32[256]{0:T(256)} %cnt_hbm.1) | copy-start | bytes 3076
  0.0 9.0 %copy-start.4 = (s32[96]{0:T(128)S(1)}, s32[96]{0:T(128)}, u32[]{:S(2)}) copy-start(s32[96]{0:T(128)} %param.11) | copy-start | bytes 1156
  0.0 0.7 copy-start.1
  0.7 0.7 copy-start.2
  6.9 5.8 %collective-permute-start = (bf16[48,128,128]{2,1,0:T(8,128)(2,1)}, bf16[48,128,128]{2,1,0:T(8,128)(2,1)S(1)}, u32[]{:S(2)}, u32[]{:S(2)}) collective-permute-start(bf16[48,128,128]{2,1,0:T(8,128)(2,1)} %get-tuple-element.7), channel_id=1, source_target_pairs={{0,1},{1,0},{2,3},{3,2},{4,5},{5,4},{6,7},{7,6},{8,9},{9,8},{10,11... | collective-permute-start | bytes 4718600 | tf_op jit(solution)/shard_map/ppermute | solution.py:158

commit v8 on v7

--- a/solution.py
+++ b/solution.py
@@ -50,8 +50,8 @@
         nb, nosv = h.shape
         h = h.reshape(nb // (4 * LANES), 4, LANES, nosv)
         h = jnp.concatenate([h[START:], h[:START]], 0)
-        even = jnp.concatenate([h[:, z].reshape(nb // 4, nosv) for z in (0, 2)], 0)
-        odd = jnp.concatenate([h[:, z].reshape(nb // 4, nosv) for z in (1, 3)], 0)
+        even = jnp.concatenate([h[:, z].reshape(nb // 4, nosv) for z in (2, 0)], 0)
+        odd = jnp.concatenate([h[:, z].reshape(nb // 4, nosv) for z in (3, 1)], 0)
         scaled[i] = jnp.concatenate([jnp.where(first, even, odd), jnp.where(first, odd, even)], 0).astype(scaled.dtype)
 
     def expand(i):
@@ -227,7 +227,7 @@
             for fixed in range(side):
                 even = line(1 - c, fixed, z, c)
                 odd = line(1 - c, fixed, (z + 1 - 2 * c) % nz, c)
-                planes.append(even + odd)
+                planes.append(odd + even)
     mine = summed(mine, both, planes)
     order = [(z + START) % (nz // 2) for z in range(nz // 2)]
     columns = [[2 * (2 * z + e) + c for z in order] for e in range(2) for c in range(2)]

time: 77.8 us -> 76.9 us (0.988)
  no operation moved by 1% of the time
where the time goes in v8:
time: 76.9 us; the launch traced here: 76.4 us
  blocking collectives  60.7 us (79%)
  Pallas kernels  9.73 us (13%)
  local copies, waits for them, and re-layouts  2.37 us (3%)
  starting transfers between devices  1.92 us (2%)
  other arithmetic  1.51 us (2%)
    all_to_all x3, blocking collectives, summed(): lax.all_to_all(tiles, axes, 0, 0, tiled=True, axis_index_groups=groups)  60.7 us
    pallas_call x1, Pallas kernels, local(): pl.pallas_call(functools.partial(amplitudes, kdom, tile), in_specs=[smem,...  5.46 us
    pallas_call x1, Pallas kernels, local(): pl.pallas_call(functools.partial(place_own, side * each), in_specs=[smem,...  1.95 us
    ppermute x1, starting transfers between devices, local(): got = lax.ppermute(sent, 'occ', [(i, i ^ 1) for i in range(nocc)])  1.92 us
    pallas_call x1, Pallas kernels, local(): pl.pallas_call(functools.partial(place_got, side * each), in_specs=[smem,...  1.7 us
  transfers between devices with their start and end apart: 1, of which 0 were waited for; matrix products, arithmetic and copies ran while one was open for 2% of the time, Pallas kernels for 3%

profile of v8, /device:TPU:6, one launch (start us, length us, event | category | flops | bytes accessed | tf_op | source)
XLA Modules:
  0.0 76.4 jit_solution(12271698359395486445)
XLA Ops:
  0.0 0.0 copy-start
  0.0 0.0 copy-start.3
  0.0 0.0 copy-start.4
  0.0 0.0 copy-start.1
  0.0 0.7 copy-done.1
  0.7 0.0 copy-start.2
  0.7 0.7 copy-done.2
  1.4 5.5 %amplitudes.1 = (bf16[48,128,128]{2,1,0:T(8,128)(2,1)S(1)}, bf16[48,128,128]{2,1,0:T(8,128)(2,1)}) custom-call(s32[1]{0:T(128)} %bitcast.2.me_ref, s32[256]{0:T(256)S(1)} %copy-done.2, bf16[8,768,256]{2,1,0:T(8,128)(2,1)} %b_hbm.1, bf16[8,768,128]{2,1,0:T(8,128)(2,1)} %q_hbm.1, f32[8,128]{1,0:T(8,128)S(1)} %copy-done.1), custom_call_target="tpu_custom_call" | custom-call | flops 805306368 | bytes 8388608 | tf_op jit(solution)/shard_map/amplitudes/pallas_call | solution.py:138
  6.9 1.9 %collective-permute-start = (bf16[48,128,128]{2,1,0:T(8,128)(2,1)}, bf16[48,128,128]{2,1,0:T(8,128)(2,1)S(1)}, u32[]{:S(2)}, u32[]{:S(2)}) collective-permute-start(bf16[48,128,128]{2,1,0:T(8,128)(2,1)} %get-tuple-element.7), channel_id=1, source_target_pairs={{0,1},{1,0},{2,3},{3,2},{4,5},{5,4},{6,7},{7,6},{8,9},{9,8},{10,11... | collective-permute-start | bytes 4718600 | tf_op jit(solution)/shard_map/ppermute | solution.py:158
  8.8 0.0 copy-done.3
  8.8 0.1 dynamic_slice.6
  8.9 0.0 copy-done
  8.9 0.1 constant_dynamic-slice_fusion
  9.0 0.0 copy-done.4
  9.0 0.2 select_reduce_fusion.1
  9.3 0.1 lt.98
  9.4 0.1 copy.12
  9.4 0.1 reduce_sum.36
  9.5 0.1 lt.110
  9.6 0.1 lt.95
  9.7 0.1 fusion.10
  9.8 0.1 pad_add_fusion
  9.8 0.1 copy.13
  9.9 0.1 concatenate.7
  10.0 0.1 lt.99
  10.1 0.1 lt.100
  10.2 0.2 fusion
  10.4 0.2 select_reduce_fusion
  10.6 1.9 %place_own.1.base_ref = bf16[192,64,128]{2,1,0:T(8,128)(2,1)S(1)} custom-call(s32[48]{0:T(128)S(1)} %get-tuple-element.18.heads, s32[48]{0:T(128)S(1)} %get-tuple-element.13.after, bf16[48,128,128]{2,1,0:T(8,128)(2,1)S(1)} %get-tuple-element.8.own_ref), custom_call_target="tpu_custom_call" | custom-call | flops 2097152 | bytes 2097152 | tf_op jit(solution)/shard_map/place_own/pallas_call | solution.py:180
  12.6 0.0 collective-permute-done.got_ref
  12.6 1.7 %place_got.1 = bf16[192,64,128]{2,1,0:T(8,128)(2,1)S(1)} custom-call(s32[48]{0:T(128)S(1)} %get-tuple-element.17.heads, s32[48]{0:T(128)S(1)} %get-tuple-element.14.after, bf16[48,128,128]{2,1,0:T(8,128)(2,1)S(1)} %collective-permute-done.got_ref, bf16[192,64,128]{2,1,0:T(8,128)(2,1)S(1)} %place_own.1.base_ref), custom_call_target="tpu_custom_call", output_to_operand_aliasing={{}: (3, {})} | custom-call | tf_op jit(solution)/shard_map/place_got/pallas_call | solution.py:189
  14.3 28.9 %all_to_all.15 = bf16[192,64,128]{2,1,0:T(8,128)(2,1)S(1)} all-to-all(bf16[192,64,128]{2,1,0:T(8,128)(2,1)S(1)} %place_got.1), channel_id=1, replica_groups={{256,384,0,128},{288,416,32,160},{320,448,64,192},{352,480,96,224},{258..., dimensions={0} | all-to-all | bytes 6291456 | tf_op jit(solution)/shard_map/all_to_all | solution.py:207
  43.2 0.6 add_parts.1
  43.8 12.0 %all_to_all.16 = bf16[48,64,128]{2,1,0:T(8,128)(2,1)S(1)} all-to-all(bf16[48,64,128]{2,1,0:T(8,128)(2,1)S(1)} %add_parts.1), channel_id=1, replica_groups={{66,98,2,34,64,96,0,32},{194,226,130,162,192,224,128,160},{322,354,258,..., dimensions={0} | all-to-all | bytes 1572864 | tf_op jit(solution)/shard_map/all_to_all | solution.py:207
  55.8 0.1 reduce_sum.37
  56.0 19.8 %all_to_all.17 = bf16[48,8,128]{2,1,0:T(8,128)(2,1)S(1)} all-to-all(bf16[48,8,128]{2,1,0:T(8,128)(2,1)S(1)} %bitcast.23), channel_id=1, replica_groups={{20,24,28,0,4,8,12,16},{21,25,29,1,5,9,13,17},{22,26,30,2,6,10,14,18},{..., dimensions={0} | all-to-all | bytes 196608 | tf_op jit(solution)/shard_map/all_to_all | solution.py:207
  75.8 0.6 reduce_sum.38
  (10 shorter events, 0.1 us)
Async XLA Ops:
  0.0 8.9 %copy-start = (s32[256,6]{0,1:T(8,128)S(1)}, s32[256,6]{0,1:T(8,128)}, u32[]{:S(2)}) copy-start(s32[256,6]{0,1:T(8,128)} %param.9) | copy-start | bytes 18436
  0.0 8.8 %copy-start.3 = (s32[256]{0:T(256)S(1)}, s32[256]{0:T(256)}, u32[]{:S(2)}) copy-start(s32[256]{0:T(256)} %cnt_hbm.1) | copy-start | bytes 3076
  0.0 9.0 %copy-start.4 = (s32[96]{0:T(128)S(1)}, s32[96]{0:T(128)}, u32[]{:S(2)}) copy-start(s32[96]{0:T(128)} %param.11) | copy-start | bytes 1156
  0.0 0.7 copy-start.1
  0.7 0.7 copy-start.2
  6.9 5.7 %collective-permute-start = (bf16[48,128,128]{2,1,0:T(8,128)(2,1)}, bf16[48,128,128]{2,1,0:T(8,128)(2,1)S(1)}, u32[]{:S(2)}, u32[]{:S(2)}) collective-permute-start(bf16[48,128,128]{2,1,0:T(8,128)(2,1)} %get-tuple-element.7), channel_id=1, source_target_pairs={{0,1},{1,0},{2,3},{3,2},{4,5},{5,4},{6,7},{7,6},{8,9},{9,8},{10,11... | collective-permute-start | bytes 4718600 | tf_op jit(solution)/shard_map/ppermute | solution.py:158

commit v9 on v8

--- a/solution.py
+++ b/solution.py
@@ -10,7 +10,7 @@
 
 LANES = 8
 TURN = 2
-START = 5
+START = 4
 
 
 def amplitudes(kdom, tile, me_ref, cnt_hbm, b_hbm, q_hbm, inv_hbm, keep_ref, send_hbm, cnt, b_buf, q_buf, inv, scaled, send_ref, small, sems):

time: 76.9 us -> 76.6 us (level)
  blocking collectives: 60.7 us -> 59.9 us
    all_to_all x3, blocking collectives: 60.7 us -> 59.9 us  [summed(): lax.all_to_all(tiles, axes, 0, 0, tiled=True, axis_index_groups=groups)]
where the time goes in v9:
time: 76.6 us; the launch traced here: 75.7 us
  blocking collectives  59.9 us (78%)
  Pallas kernels  9.79 us (13%)
  local copies, waits for them, and re-layouts  2.37 us (3%)
  starting transfers between devices  1.92 us (3%)
  other arithmetic  1.51 us (2%)
    all_to_all x3, blocking collectives, summed(): lax.all_to_all(tiles, axes, 0, 0, tiled=True, axis_index_groups=groups)  59.9 us
    pallas_call x1, Pallas kernels, local(): pl.pallas_call(functools.partial(amplitudes, kdom, tile), in_specs=[smem,...  5.46 us
    pallas_call x1, Pallas kernels, local(): pl.pallas_call(functools.partial(place_own, side * each), in_specs=[smem,...  2.01 us
    ppermute x1, starting transfers between devices, local(): got = lax.ppermute(sent, 'occ', [(i, i ^ 1) for i in range(nocc)])  1.92 us
    pallas_call x1, Pallas kernels, local(): pl.pallas_call(functools.partial(place_got, side * each), in_specs=[smem,...  1.69 us
  transfers between devices with their start and end apart: 1, of which 0 were waited for; matrix products, arithmetic and copies ran while one was open for 2% of the time, Pallas kernels for 3%

profile of v9, /device:TPU:6, one launch (start us, length us, event | category | flops | bytes accessed | tf_op | source)
XLA Modules:
  0.0 75.7 jit_solution(12272675850876980423)
XLA Ops:
  0.0 0.0 copy-start
  0.0 0.0 copy-start.3
  0.0 0.0 copy-start.4
  0.0 0.0 copy-start.1
  0.0 0.7 copy-done.1
  0.7 0.0 copy-start.2
  0.7 0.7 copy-done.2
  1.4 5.5 %amplitudes.1 = (bf16[48,128,128]{2,1,0:T(8,128)(2,1)S(1)}, bf16[48,128,128]{2,1,0:T(8,128)(2,1)}) custom-call(s32[1]{0:T(128)} %bitcast.2.me_ref, s32[256]{0:T(256)S(1)} %copy-done.2, bf16[8,768,256]{2,1,0:T(8,128)(2,1)} %b_hbm.1, bf16[8,768,128]{2,1,0:T(8,128)(2,1)} %q_hbm.1, f32[8,128]{1,0:T(8,128)S(1)} %copy-done.1), custom_call_target="tpu_custom_call" | custom-call | flops 805306368 | bytes 8388608 | tf_op jit(solution)/shard_map/amplitudes/pallas_call | solution.py:138
  6.9 1.9 %collective-permute-start = (bf16[48,128,128]{2,1,0:T(8,128)(2,1)}, bf16[48,128,128]{2,1,0:T(8,128)(2,1)S(1)}, u32[]{:S(2)}, u32[]{:S(2)}) collective-permute-start(bf16[48,128,128]{2,1,0:T(8,128)(2,1)} %get-tuple-element.7), channel_id=1, source_target_pairs={{0,1},{1,0},{2,3},{3,2},{4,5},{5,4},{6,7},{7,6},{8,9},{9,8},{10,11... | collective-permute-start | bytes 4718600 | tf_op jit(solution)/shard_map/ppermute | solution.py:158
  8.8 0.0 copy-done.3
  8.8 0.1 dynamic_slice.6
  8.9 0.0 copy-done
  8.9 0.1 constant_dynamic-slice_fusion
  9.0 0.0 copy-done.4
  9.0 0.2 select_reduce_fusion.1
  9.3 0.1 lt.98
  9.4 0.1 copy.12
  9.4 0.1 reduce_sum.36
  9.5 0.1 lt.110
  9.6 0.1 lt.95
  9.7 0.1 fusion.10
  9.8 0.1 pad_add_fusion
  9.8 0.1 copy.13
  9.9 0.1 concatenate.7
  10.0 0.1 lt.99
  10.1 0.1 lt.100
  10.2 0.2 fusion
  10.4 0.2 select_reduce_fusion
  10.6 2.0 %place_own.1.base_ref = bf16[192,64,128]{2,1,0:T(8,128)(2,1)S(1)} custom-call(s32[48]{0:T(128)S(1)} %get-tuple-element.18.heads, s32[48]{0:T(128)S(1)} %get-tuple-element.13.after, bf16[48,128,128]{2,1,0:T(8,128)(2,1)S(1)} %get-tuple-element.8.own_ref), custom_call_target="tpu_custom_call" | custom-call | flops 2097152 | bytes 2097152 | tf_op jit(solution)/shard_map/place_own/pallas_call | solution.py:180
  12.6 0.0 collective-permute-done.got_ref
  12.7 1.7 %place_got.1 = bf16[192,64,128]{2,1,0:T(8,128)(2,1)S(1)} custom-call(s32[48]{0:T(128)S(1)} %get-tuple-element.17.heads, s32[48]{0:T(128)S(1)} %get-tuple-element.14.after, bf16[48,128,128]{2,1,0:T(8,128)(2,1)S(1)} %collective-permute-done.got_ref, bf16[192,64,128]{2,1,0:T(8,128)(2,1)S(1)} %place_own.1.base_ref), custom_call_target="tpu_custom_call", output_to_operand_aliasing={{}: (3, {})} | custom-call | tf_op jit(solution)/shard_map/place_got/pallas_call | solution.py:189
  14.4 28.8 %all_to_all.15 = bf16[192,64,128]{2,1,0:T(8,128)(2,1)S(1)} all-to-all(bf16[192,64,128]{2,1,0:T(8,128)(2,1)S(1)} %place_got.1), channel_id=1, replica_groups={{256,384,0,128},{288,416,32,160},{320,448,64,192},{352,480,96,224},{258..., dimensions={0} | all-to-all | bytes 6291456 | tf_op jit(solution)/shard_map/all_to_all | solution.py:207
  43.1 0.6 add_parts.1
  43.8 12.0 %all_to_all.16 = bf16[48,64,128]{2,1,0:T(8,128)(2,1)S(1)} all-to-all(bf16[48,64,128]{2,1,0:T(8,128)(2,1)S(1)} %add_parts.1), channel_id=1, replica_groups={{66,98,2,34,64,96,0,32},{194,226,130,162,192,224,128,160},{322,354,258,..., dimensions={0} | all-to-all | bytes 1572864 | tf_op jit(solution)/shard_map/all_to_all | solution.py:207
  55.8 0.1 reduce_sum.37
  55.9 19.1 %all_to_all.17 = bf16[48,8,128]{2,1,0:T(8,128)(2,1)S(1)} all-to-all(bf16[48,8,128]{2,1,0:T(8,128)(2,1)S(1)} %bitcast.23), channel_id=1, replica_groups={{16,20,24,28,0,4,8,12},{17,21,25,29,1,5,9,13},{18,22,26,30,2,6,10,14},{..., dimensions={0} | all-to-all | bytes 196608 | tf_op jit(solution)/shard_map/all_to_all | solution.py:207
  75.1 0.6 reduce_sum.38
  (10 shorter events, 0.1 us)
Async XLA Ops:
  0.0 8.9 %copy-start = (s32[256,6]{0,1:T(8,128)S(1)}, s32[256,6]{0,1:T(8,128)}, u32[]{:S(2)}) copy-start(s32[256,6]{0,1:T(8,128)} %param.9) | copy-start | bytes 18436
  0.0 8.8 %copy-start.3 = (s32[256]{0:T(256)S(1)}, s32[256]{0:T(256)}, u32[]{:S(2)}) copy-start(s32[256]{0:T(256)} %cnt_hbm.1) | copy-start | bytes 3076
  0.0 9.0 %copy-start.4 = (s32[96]{0:T(128)S(1)}, s32[96]{0:T(128)}, u32[]{:S(2)}) copy-start(s32[96]{0:T(128)} %param.11) | copy-start | bytes 1156
  0.0 0.7 copy-start.1
  0.7 0.7 copy-start.2
  6.9 5.8 %collective-permute-start = (bf16[48,128,128]{2,1,0:T(8,128)(2,1)}, bf16[48,128,128]{2,1,0:T(8,128)(2,1)S(1)}, u32[]{:S(2)}, u32[]{:S(2)}) collective-permute-start(bf16[48,128,128]{2,1,0:T(8,128)(2,1)} %get-tuple-element.7), channel_id=1, source_target_pairs={{0,1},{1,0},{2,3},{3,2},{4,5},{5,4},{6,7},{7,6},{8,9},{9,8},{10,11... | collective-permute-start | bytes 4718600 | tf_op jit(solution)/shard_map/ppermute | solution.py:158
